TPU v7x, 256 devices: a whole 4x4x8 slice. The times are simulated.
256 devices in a mesh: gx: 8 (over z), gy: 16 (over y, x), gz: 2 (over core).
Axes of the slice: x: 4, y: 4, z: 8, core: 2. Of those that a mesh axis runs over, the one named last changes fastest.
Arguments:
- right_side: float32 [128, 512, 1024], P('gx', 'gy', 'gz'), may hold values from -6 to 6
- coefficient: float32 [128, 512, 1024], P('gx', 'gy', 'gz'), may hold values from 0.2 to 5
Outputs:
- solution_field: float32 [128, 512, 1024], P('gx', 'gy', 'gz')
All inputs are finite; a program needn't handle non-finite values.
Results may differ from a plain program's by a relative error of at most 0.0003.
Values sent between devices are 32-bit elements; how exact they have to be, the bound alone decides.
A program may use at most 192 MiB of HBM per device.

v0:
```python
import jax
import jax.numpy as jnp
from jax import lax
from jax.sharding import PartitionSpec as P

SWEEPS = 2
BOTTOM_SWEEPS = 6


def padded_2(cells, sides, width):
    for axis, dim in sides:
        count = lax.axis_size(axis)
        ends = count - 1
        head = lax.slice_in_dim(cells, 0, width, axis=dim)
        tail = lax.slice_in_dim(cells, cells.shape[dim] - width, cells.shape[dim], axis=dim)
        cells = jnp.concatenate(
            [
                lax.ppermute(tail, axis, [(i, (i + 1) % count) for i in range(ends)]),
                cells,
                lax.ppermute(head, axis, [((i + 1) % count, i) for i in range(ends)]),
            ],
            axis=dim,
        )
    return cells


def neighbour(padded, which_dim, offset):
    window_list = [slice(1, -1)] * 3
    window_list[which_dim] = slice(offset, offset + padded.shape[which_dim] - 2)
    return padded[tuple(window_list)]


def operator_of(coefficient, padded, level_scale):
    face_list = []
    for which_dim in range(3):
        for offset in (0, 2):
            beside = neighbour(padded, which_dim, offset)
            face_list.append(
                level_scale * jnp.where(beside > 0.0, 0.5 * (coefficient + beside), coefficient)
            )
    diagonal = face_list[0]
    for weight in face_list[1:]:
        diagonal = diagonal + weight
    return (face_list, diagonal)


def apply_op(padded, values, operator):
    face_list, diagonal = operator
    result = diagonal * values
    number = 0
    for which_dim in range(3):
        for offset in (0, 2):
            result = result - face_list[number] * neighbour(padded, which_dim, offset)
            number += 1
    return result


def chebyshev(
    rhs_field, initial, sweeps, lower_edge, upper_edge, extend, operator, initial_padded=None
):
    cheb_theta = 0.5 * (upper_edge + lower_edge)
    cheb_delta = 0.5 * (upper_edge - lower_edge)
    cheb_sigma = cheb_theta / cheb_delta
    cheb_rho = 1.0 / cheb_sigma
    diagonal = operator[1]
    if initial is None:
        remain = rhs_field
        iterate = jnp.zeros_like(rhs_field)
    else:
        initial_padded = extend(initial)
        remain = rhs_field - apply_op(initial_padded, initial, operator)
        iterate = initial
    step_dir = remain / diagonal * (1.0 / cheb_theta)
    iterate = iterate + step_dir
    for sweep in range(1, sweeps):
        rho_next = 1.0 / (2.0 * cheb_sigma - cheb_rho)
        remain = rhs_field - apply_op(extend(iterate), iterate, operator)
        step_dir = rho_next * cheb_rho * step_dir + 2.0 * rho_next / cheb_delta * (
            remain / diagonal
        )
        iterate = iterate + step_dir
        cheb_rho = rho_next
    return iterate


def coarsen(coefficient):
    dims_now = coefficient.shape
    blocks = coefficient.reshape(dims_now[0] // 2, 2, dims_now[1] // 2, 2, dims_now[2] // 2, 2)
    return jnp.mean(blocks, axis=(1, 3, 5))


def restrict_along(padded, which_dim):
    dims_now = padded.shape
    paired = padded.reshape(
        dims_now[:which_dim] + (dims_now[which_dim] // 2, 2) + dims_now[which_dim + 1 :]
    )
    length = paired.shape[which_dim]
    first_part = lax.index_in_dim(paired, 0, which_dim + 1, keepdims=False)
    second = lax.index_in_dim(paired, 1, which_dim + 1, keepdims=False)
    return 0.125 * (
        lax.slice_in_dim(first_part, 0, length - 1, axis=which_dim)
        + 3.0 * lax.slice_in_dim(second, 0, length - 1, axis=which_dim)
        + 3.0 * lax.slice_in_dim(first_part, 1, length, axis=which_dim)
        + lax.slice_in_dim(second, 1, length, axis=which_dim)
    )


def restrict_all(padded):
    for which_dim in range(3):
        padded = restrict_along(padded, which_dim)
    return padded


def prolong_along(padded, which_dim):
    length = padded.shape[which_dim] - 2
    centre = lax.slice_in_dim(padded, 1, length + 1, axis=which_dim)
    lower_cell = lax.slice_in_dim(padded, 0, length, axis=which_dim)
    upper_cell = lax.slice_in_dim(padded, 2, length + 2, axis=which_dim)
    even_cells = 0.75 * centre + 0.25 * lower_cell
    odd_cells = 0.75 * centre + 0.25 * upper_cell
    joined = jnp.stack((even_cells, odd_cells), axis=which_dim + 1)
    dims_now = joined.shape
    return joined.reshape(dims_now[:which_dim] + (2 * length,) + dims_now[which_dim + 2 :])


def prolong_all(padded):
    for which_dim in range(3):
        padded = prolong_along(padded, which_dim)
    return padded


def pad_block(values):
    return padded_2(values, (("gx", 0), ("gy", 1), ("gz", 2)), 1)


def pad_corners(values):
    return padded_2(values, (("gx", 0), ("gy", 1), ("gz", 2)), 1)


def local(right_side, coefficient):
    coarse_one = coarsen(coefficient)
    coarse_two = coarsen(coarse_one)
    fine_ops = operator_of(coefficient, pad_block(coefficient), 1.0)
    mid_ops = operator_of(coarse_one, pad_block(coarse_one), 0.25)
    pre_fine = chebyshev(right_side, None, SWEEPS, 0.3, 2.0, pad_block, fine_ops)
    resid_fine = right_side - apply_op(pad_block(pre_fine), pre_fine, fine_ops)
    mid_rhs = restrict_all(pad_corners(resid_fine))
    pre_mid = chebyshev(mid_rhs, None, SWEEPS, 0.3, 2.0, pad_block, mid_ops)
    resid_mid = mid_rhs - apply_op(pad_block(pre_mid), pre_mid, mid_ops)
    low_rhs = restrict_all(pad_corners(resid_mid))
    low_ops = operator_of(coarse_two, pad_block(coarse_two), 0.0625)
    bottom = chebyshev(low_rhs, None, BOTTOM_SWEEPS, 0.05, 2.0, pad_block, low_ops)
    post_mid = chebyshev(
        mid_rhs, pre_mid + prolong_all(pad_corners(bottom)), SWEEPS, 0.3, 2.0, pad_block, mid_ops
    )
    return chebyshev(
        right_side,
        pre_fine + prolong_all(pad_corners(post_mid)),
        SWEEPS,
        0.3,
        2.0,
        pad_block,
        fine_ops,
    )


def solution(mesh):
    return jax.shard_map(
        local,
        mesh=mesh,
        in_specs=(P("gx", "gy", "gz"), P("gx", "gy", "gz")),
        out_specs=P("gx", "gy", "gz"),
        check_vma=False,
    )
```

profile of v0, /device:TPU:137, one launch (start us, length us, event | category | flops | bytes accessed | tf_op | source)
XLA Modules:
  0.0 650.4 jit_solution(13101292492643715209)
XLA Ops:
  19.0 4.8 collective-permute-start.5
  28.5 5.1 collective-permute-start.7
  39.8 6.1 collective-permute-start.9
  47.8 4.9 collective-permute-done.8
  52.9 5.2 collective-permute-start.11
  71.2 68.4 %reshape.71 = f32[8,2,16,2,256,2]{5,4,3,2,1,0:T(8,128)} reshape(f32[16,32,512]{2,1,0:T(8,128)S(1)} %copy-done) | data formatting | bytes 2097152 | tf_op jit(solution)/shard_map/reshape | solution.py:88
  139.5 21.4 %reduce_sum.18 = f32[8,16,256]{2,1,0:T(8,128)} reduce(f32[8,2,16,2,256,2]{5,4,3,2,1,0:T(8,128)} %reshape.71, f32[]{:T(128)} %constant.21.clone.1), dimensions={1,3,5}, to_apply=%region_0.0 | reduce | flops 229376 | bytes 1179652 | tf_op jit(solution)/shard_map/reduce_sum | solution.py:89
  170.9 4.5 collective-permute-start.17
  179.3 4.8 collective-permute-start.25
  184.0 9.7 %div.57 = f32[4,2,8,2,128,2]{5,4,3,2,1,0:T(8,128)} reshape(f32[8,16,256]{2,1,0:T(8,128)S(1)} %broadcast_multiply_fusion) | data formatting | bytes 262144 | tf_op jit(solution)/shard_map/div | solution.py:89
  193.7 4.6 reduce_sum.19
  198.4 5.6 fusion.33
  211.3 5.5 collective-permute-start.27
  225.8 6.6 %collective-permute-start.23 = (f32[18,34,1]{2,1,0:T(8,128)S(1)}, f32[18,34,1]{2,1,0:T(8,128)S(1)}, u32[]{:S(2)}, u32[]{:S(2)}) collective-permute-start(f32[18,34,1]{2,1,0:T(8,128)S(1)} %get-tuple-element.39), channel_id=1, source_target_pairs={{1,0},{3,2},{5,4},{7,6},{9,8},{11,10},{13,12},{15,14},{17,16},{19,... | collective-permute-start | bytes 7352 | tf_op jit(solution)/shard_map/ppermute | solution.py:20
  235.8 4.3 collective-permute-start.29
  270.7 4.6 collective-permute-start.49
  290.2 5.5 collective-permute-start.51
  304.3 4.3 collective-permute-start.41
  356.8 5.5 collective-permute-start.57
  364.4 4.4 collective-permute-start.59
  379.9 6.0 collective-permute-start.63
  404.9 4.5 collective-permute-start.69
  427.7 4.5 collective-permute-start.75
  450.5 4.5 collective-permute-start.81
  473.3 4.5 collective-permute-start.87
  503.5 6.0 collective-permute-start.93
  511.4 4.6 collective-permute-done.92
  516.1 4.7 collective-permute-start.95
  541.6 4.4 collective-permute-start.101
  565.8 4.4 collective-permute-start.107
  579.9 5.3 copy.235
  645.4 4.9 fusion.6
  (462 shorter events, 403.8 us)
Async XLA Ops:
  39.8 8.0 %collective-permute-start.9 = (f32[18,1,512]{2,1,0:T(1,128)S(1)}, f32[18,1,512]{2,1,0:T(1,128)S(1)}, u32[]{:S(2)}, u32[]{:S(2)}) collective-permute-start(f32[18,1,512]{2,1,0:T(1,128)S(1)} %get-tuple-element.55), channel_id=1, source_target_pairs={{2,0},{4,2},{6,4},{8,6},{10,8},{12,10},{14,12},{16,14},{18,16},{20... | collective-permute-start | bytes 110600 | tf_op jit(solution)/shard_map/ppermute | solution.py:20
  65.9 95.1 %collective-permute-start.13 = (f32[1,32,512]{2,1,0:T(8,128)S(1)}, f32[1,32,512]{2,1,0:T(8,128)S(1)}, u32[]{:S(2)}, u32[]{:S(2)}) collective-permute-start(f32[1,32,512]{2,1,0:T(8,128)S(1)} %get-tuple-element.65), channel_id=1, source_target_pairs={{32,0},{64,32},{96,64},{128,96},{160,128},{192,160},{224,192},{33,... | collective-permute-start | bytes 196616 | tf_op jit(solution)/shard_map/ppermute | solution.py:20
  67.8 93.2 %collective-permute-start.12 = (f32[1,32,512]{2,1,0:T(8,128)S(1)}, f32[1,32,512]{2,1,0:T(8,128)S(1)}, u32[]{:S(2)}, u32[]{:S(2)}) collective-permute-start(f32[1,32,512]{2,1,0:T(8,128)S(1)} %get-tuple-element.64), channel_id=1, source_target_pairs={{0,32},{32,64},{64,96},{96,128},{128,160},{160,192},{192,224},{1,3... | collective-permute-start | bytes 196616 | tf_op jit(solution)/shard_map/ppermute | solution.py:18
  170.9 27.4 %collective-permute-start.17 = (f32[18,34,1]{2,1,0:T(8,128)}, f32[18,34,1]{2,1,0:T(8,128)}, u32[]{:S(2)}, u32[]{:S(2)}) collective-permute-start(f32[18,34,1]{2,1,0:T(8,128)} %get-tuple-element.41), channel_id=1, source_target_pairs={{1,0},{3,2},{5,4},{7,6},{9,8},{11,10},{13,12},{15,14},{17,16},{19,... | collective-permute-start | bytes 7352 | tf_op jit(solution)/shard_map/ppermute | solution.py:20
  175.4 22.9 %collective-permute-start.16 = (f32[18,34,1]{2,1,0:T(8,128)}, f32[18,34,1]{2,1,0:T(8,128)}, u32[]{:S(2)}, u32[]{:S(2)}) collective-permute-start(f32[18,34,1]{2,1,0:T(8,128)} %get-tuple-element.40), channel_id=1, source_target_pairs={{0,1},{2,3},{4,5},{6,7},{8,9},{10,11},{12,13},{14,15},{16,17},{18,... | collective-permute-start | bytes 7352 | tf_op jit(solution)/shard_map/ppermute | solution.py:18
  177.3 32.0 %collective-permute-start.24 = (f32[1,16,256]{2,1,0:T(8,128)}, f32[1,16,256]{2,1,0:T(8,128)S(1)}, u32[]{:S(2)}, u32[]{:S(2)}) collective-permute-start(f32[1,16,256]{2,1,0:T(8,128)} %get-tuple-element.123), channel_id=1, source_target_pairs={{0,32},{32,64},{64,96},{96,128},{128,160},{160,192},{192,224},{1,3... | collective-permute-start | bytes 49160 | tf_op jit(solution)/shard_map/ppermute | solution.py:18
  179.3 30.0 %collective-permute-start.25 = (f32[1,16,256]{2,1,0:T(8,128)}, f32[1,16,256]{2,1,0:T(8,128)S(1)}, u32[]{:S(2)}, u32[]{:S(2)}) collective-permute-start(f32[1,16,256]{2,1,0:T(8,128)} %get-tuple-element.122), channel_id=1, source_target_pairs={{32,0},{64,32},{96,64},{128,96},{160,128},{192,160},{224,192},{33,... | collective-permute-start | bytes 49160 | tf_op jit(solution)/shard_map/ppermute | solution.py:20
  204.0 12.8 %collective-permute-start.19 = (f32[1,32,512]{2,1,0:T(8,128)S(1)}, f32[1,32,512]{2,1,0:T(8,128)S(1)}, u32[]{:S(2)}, u32[]{:S(2)}) collective-permute-start(f32[1,32,512]{2,1,0:T(8,128)S(1)} %get-tuple-element.63), channel_id=1, source_target_pairs={{32,0},{64,32},{96,64},{128,96},{160,128},{192,160},{224,192},{33,... | collective-permute-start | bytes 196616 | tf_op jit(solution)/shard_map/ppermute | solution.py:20
  205.9 10.9 %collective-permute-start.18 = (f32[1,32,512]{2,1,0:T(8,128)S(1)}, f32[1,32,512]{2,1,0:T(8,128)S(1)}, u32[]{:S(2)}, u32[]{:S(2)}) collective-permute-start(f32[1,32,512]{2,1,0:T(8,128)S(1)} %get-tuple-element.62), channel_id=1, source_target_pairs={{0,32},{32,64},{64,96},{96,128},{128,160},{160,192},{192,224},{1,3... | collective-permute-start | bytes 196616 | tf_op jit(solution)/shard_map/ppermute | solution.py:18
  209.3 12.8 %collective-permute-start.26 = (f32[10,1,256]{2,1,0:T(1,128)S(1)}, f32[10,1,256]{2,1,0:T(1,128)S(1)}, u32[]{:S(2)}, u32[]{:S(2)}) collective-permute-start(f32[10,1,256]{2,1,0:T(1,128)S(1)} %get-tuple-element.107), channel_id=1, source_target_pairs={{0,2},{2,4},{4,6},{6,8},{8,10},{10,12},{12,14},{14,16},{16,18},{18... | collective-permute-start | bytes 30728 | tf_op jit(solution)/shard_map/ppermute | solution.py:18
  211.3 10.9 %collective-permute-start.27 = (f32[10,1,256]{2,1,0:T(1,128)S(1)}, f32[10,1,256]{2,1,0:T(1,128)S(1)}, u32[]{:S(2)}, u32[]{:S(2)}) collective-permute-start(f32[10,1,256]{2,1,0:T(1,128)S(1)} %get-tuple-element.106), channel_id=1, source_target_pairs={{2,0},{4,2},{6,4},{8,6},{10,8},{12,10},{14,12},{16,14},{18,16},{20... | collective-permute-start | bytes 30728 | tf_op jit(solution)/shard_map/ppermute | solution.py:20
  225.8 14.3 %collective-permute-start.23 = (f32[18,34,1]{2,1,0:T(8,128)S(1)}, f32[18,34,1]{2,1,0:T(8,128)S(1)}, u32[]{:S(2)}, u32[]{:S(2)}) collective-permute-start(f32[18,34,1]{2,1,0:T(8,128)S(1)} %get-tuple-element.39), channel_id=1, source_target_pairs={{1,0},{3,2},{5,4},{7,6},{9,8},{11,10},{13,12},{15,14},{17,16},{19,... | collective-permute-start | bytes 7352 | tf_op jit(solution)/shard_map/ppermute | solution.py:20
  232.4 7.7 %collective-permute-start.22 = (f32[18,34,1]{2,1,0:T(8,128)S(1)}, f32[18,34,1]{2,1,0:T(8,128)S(1)}, u32[]{:S(2)}, u32[]{:S(2)}) collective-permute-start(f32[18,34,1]{2,1,0:T(8,128)S(1)} %get-tuple-element.38), channel_id=1, source_target_pairs={{0,1},{2,3},{4,5},{6,7},{8,9},{10,11},{12,13},{14,15},{16,17},{18,... | collective-permute-start | bytes 7352 | tf_op jit(solution)/shard_map/ppermute | solution.py:18
  234.5 18.6 %collective-permute-start.28 = (f32[10,18,1]{2,1,0:T(8,128)}, f32[10,18,1]{2,1,0:T(8,128)}, u32[]{:S(2)}, u32[]{:S(2)}) collective-permute-start(f32[10,18,1]{2,1,0:T(8,128)} %get-tuple-element.93), channel_id=1, source_target_pairs={{0,1},{2,3},{4,5},{6,7},{8,9},{10,11},{12,13},{14,15},{16,17},{18,... | collective-permute-start | bytes 2168 | tf_op jit(solution)/shard_map/ppermute | solution.py:18
  235.8 17.3 %collective-permute-start.29 = (f32[10,18,1]{2,1,0:T(8,128)}, f32[10,18,1]{2,1,0:T(8,128)}, u32[]{:S(2)}, u32[]{:S(2)}) collective-permute-start(f32[10,18,1]{2,1,0:T(8,128)} %get-tuple-element.92), channel_id=1, source_target_pairs={{1,0},{3,2},{5,4},{7,6},{9,8},{11,10},{13,12},{15,14},{17,16},{19,... | collective-permute-start | bytes 2168 | tf_op jit(solution)/shard_map/ppermute | solution.py:20
  263.4 11.8 %collective-permute-start.33 = (f32[10,1,256]{2,1,0:T(1,128)S(1)}, f32[10,1,256]{2,1,0:T(1,128)S(1)}, u32[]{:S(2)}, u32[]{:S(2)}) collective-permute-start(f32[10,1,256]{2,1,0:T(1,128)S(1)} %get-tuple-element.105), channel_id=1, source_target_pairs={{2,0},{4,2},{6,4},{8,6},{10,8},{12,10},{14,12},{16,14},{18,16},{20... | collective-permute-start | bytes 30728 | tf_op jit(solution)/shard_map/ppermute | solution.py:20
  265.4 9.9 %collective-permute-start.32 = (f32[10,1,256]{2,1,0:T(1,128)S(1)}, f32[10,1,256]{2,1,0:T(1,128)S(1)}, u32[]{:S(2)}, u32[]{:S(2)}) collective-permute-start(f32[10,1,256]{2,1,0:T(1,128)S(1)} %get-tuple-element.104), channel_id=1, source_target_pairs={{0,2},{2,4},{4,6},{6,8},{8,10},{10,12},{12,14},{14,16},{16,18},{18... | collective-permute-start | bytes 30728 | tf_op jit(solution)/shard_map/ppermute | solution.py:18
  268.7 11.2 %collective-permute-start.48 = (f32[1,8,128]{2,1,0:T(8,128)S(1)}, f32[1,8,128]{2,1,0:T(8,128)S(1)}, u32[]{:S(2)}, u32[]{:S(2)}) collective-permute-start(f32[1,8,128]{2,1,0:T(8,128)S(1)} %get-tuple-element.183), channel_id=1, source_target_pairs={{0,32},{32,64},{64,96},{96,128},{128,160},{160,192},{192,224},{1,3... | collective-permute-start | bytes 12296 | tf_op jit(solution)/shard_map/ppermute | solution.py:18
  270.7 9.3 %collective-permute-start.49 = (f32[1,8,128]{2,1,0:T(8,128)S(1)}, f32[1,8,128]{2,1,0:T(8,128)S(1)}, u32[]{:S(2)}, u32[]{:S(2)}) collective-permute-start(f32[1,8,128]{2,1,0:T(8,128)S(1)} %get-tuple-element.182), channel_id=1, source_target_pairs={{32,0},{64,32},{96,64},{128,96},{160,128},{192,160},{224,192},{33,... | collective-permute-start | bytes 12296 | tf_op jit(solution)/shard_map/ppermute | solution.py:20
  282.9 12.7 %collective-permute-start.37 = (f32[1,16,256]{2,1,0:T(8,128)S(1)}, f32[1,16,256]{2,1,0:T(8,128)S(1)}, u32[]{:S(2)}, u32[]{:S(2)}) collective-permute-start(f32[1,16,256]{2,1,0:T(8,128)S(1)} %get-tuple-element.119), channel_id=1, source_target_pairs={{32,0},{64,32},{96,64},{128,96},{160,128},{192,160},{224,192},{33,... | collective-permute-start | bytes 49160 | tf_op jit(solution)/shard_map/ppermute | solution.py:20
  284.9 10.8 %collective-permute-start.36 = (f32[1,16,256]{2,1,0:T(8,128)S(1)}, f32[1,16,256]{2,1,0:T(8,128)S(1)}, u32[]{:S(2)}, u32[]{:S(2)}) collective-permute-start(f32[1,16,256]{2,1,0:T(8,128)S(1)} %get-tuple-element.118), channel_id=1, source_target_pairs={{0,32},{32,64},{64,96},{96,128},{128,160},{160,192},{192,224},{1,3... | collective-permute-start | bytes 49160 | tf_op jit(solution)/shard_map/ppermute | solution.py:18
  288.2 12.8 %collective-permute-start.50 = (f32[6,1,128]{2,1,0:T(1,128)S(1)}, f32[6,1,128]{2,1,0:T(1,128)S(1)}, u32[]{:S(2)}, u32[]{:S(2)}) collective-permute-start(f32[6,1,128]{2,1,0:T(1,128)S(1)} %get-tuple-element.169), channel_id=1, source_target_pairs={{0,2},{2,4},{4,6},{6,8},{8,10},{10,12},{12,14},{14,16},{16,18},{18... | collective-permute-start | bytes 9224 | tf_op jit(solution)/shard_map/ppermute | solution.py:18
  290.2 27.3 %collective-permute-start.51 = (f32[6,1,128]{2,1,0:T(1,128)S(1)}, f32[6,1,128]{2,1,0:T(1,128)S(1)}, u32[]{:S(2)}, u32[]{:S(2)}) collective-permute-start(f32[6,1,128]{2,1,0:T(1,128)S(1)} %get-tuple-element.168), channel_id=1, source_target_pairs={{2,0},{4,2},{6,4},{8,6},{10,8},{12,10},{14,12},{16,14},{18,16},{20... | collective-permute-start | bytes 9224 | tf_op jit(solution)/shard_map/ppermute | solution.py:20
  320.8 10.7 %collective-permute-start.45 = (f32[10,1,256]{2,1,0:T(1,128)S(1)}, f32[10,1,256]{2,1,0:T(1,128)S(1)}, u32[]{:S(2)}, u32[]{:S(2)}) collective-permute-start(f32[10,1,256]{2,1,0:T(1,128)S(1)} %get-tuple-element.101), channel_id=1, source_target_pairs={{2,0},{4,2},{6,4},{8,6},{10,8},{12,10},{14,12},{16,14},{18,16},{20... | collective-permute-start | bytes 30728 | tf_op jit(solution)/shard_map/ppermute | solution.py:20
  322.7 8.8 %collective-permute-start.44 = (f32[10,1,256]{2,1,0:T(1,128)S(1)}, f32[10,1,256]{2,1,0:T(1,128)S(1)}, u32[]{:S(2)}, u32[]{:S(2)}) collective-permute-start(f32[10,1,256]{2,1,0:T(1,128)S(1)} %get-tuple-element.100), channel_id=1, source_target_pairs={{0,2},{2,4},{4,6},{6,8},{8,10},{10,12},{12,14},{14,16},{16,18},{18... | collective-permute-start | bytes 30728 | tf_op jit(solution)/shard_map/ppermute | solution.py:18
  326.2 9.9 %collective-permute-start.53 = (f32[6,10,1]{2,0,1:T(8,128)S(1)}, f32[6,10,1]{2,0,1:T(8,128)S(1)}, u32[]{:S(2)}, u32[]{:S(2)}) collective-permute-start(f32[6,10,1]{2,0,1:T(8,128)S(1)} %get-tuple-element.154), channel_id=1, source_target_pairs={{1,0},{3,2},{5,4},{7,6},{9,8},{11,10},{13,12},{15,14},{17,16},{19,... | collective-permute-start | bytes 728 | tf_op jit(solution)/shard_map/ppermute | solution.py:20
  377.9 8.0 %collective-permute-start.62 = (f32[6,1,128]{2,1,0:T(1,128)S(1)}, f32[6,1,128]{2,1,0:T(1,128)S(1)}, u32[]{:S(2)}, u32[]{:S(2)}) collective-permute-start(f32[6,1,128]{2,1,0:T(1,128)S(1)} %get-tuple-element.165), channel_id=1, source_target_pairs={{0,2},{2,4},{4,6},{6,8},{8,10},{10,12},{12,14},{14,16},{16,18},{18... | collective-permute-start | bytes 9224 | tf_op jit(solution)/shard_map/ppermute | solution.py:18
  401.4 8.0 %collective-permute-start.68 = (f32[6,1,128]{2,1,0:T(1,128)S(1)}, f32[6,1,128]{2,1,0:T(1,128)S(1)}, u32[]{:S(2)}, u32[]{:S(2)}) collective-permute-start(f32[6,1,128]{2,1,0:T(1,128)S(1)} %get-tuple-element.163), channel_id=1, source_target_pairs={{0,2},{2,4},{4,6},{6,8},{8,10},{10,12},{12,14},{14,16},{16,18},{18... | collective-permute-start | bytes 9224 | tf_op jit(solution)/shard_map/ppermute | solution.py:18
  424.3 8.0 %collective-permute-start.74 = (f32[6,1,128]{2,1,0:T(1,128)S(1)}, f32[6,1,128]{2,1,0:T(1,128)S(1)}, u32[]{:S(2)}, u32[]{:S(2)}) collective-permute-start(f32[6,1,128]{2,1,0:T(1,128)S(1)} %get-tuple-element.161), channel_id=1, source_target_pairs={{0,2},{2,4},{4,6},{6,8},{8,10},{10,12},{12,14},{14,16},{16,18},{18... | collective-permute-start | bytes 9224 | tf_op jit(solution)/shard_map/ppermute | solution.py:18
  447.1 8.0 %collective-permute-start.80 = (f32[6,1,128]{2,1,0:T(1,128)S(1)}, f32[6,1,128]{2,1,0:T(1,128)S(1)}, u32[]{:S(2)}, u32[]{:S(2)}) collective-permute-start(f32[6,1,128]{2,1,0:T(1,128)S(1)} %get-tuple-element.158), channel_id=1, source_target_pairs={{0,2},{2,4},{4,6},{6,8},{8,10},{10,12},{12,14},{14,16},{16,18},{18... | collective-permute-start | bytes 9224 | tf_op jit(solution)/shard_map/ppermute | solution.py:18
  469.9 8.0 %collective-permute-start.86 = (f32[6,1,128]{2,1,0:T(1,128)S(1)}, f32[6,1,128]{2,1,0:T(1,128)S(1)}, u32[]{:S(2)}, u32[]{:S(2)}) collective-permute-start(f32[6,1,128]{2,1,0:T(1,128)S(1)} %get-tuple-element.157), channel_id=1, source_target_pairs={{0,2},{2,4},{4,6},{6,8},{8,10},{10,12},{12,14},{14,16},{16,18},{18... | collective-permute-start | bytes 9224 | tf_op jit(solution)/shard_map/ppermute | solution.py:18
  503.5 8.0 %collective-permute-start.93 = (f32[10,1,256]{2,1,0:T(1,128)S(1)}, f32[10,1,256]{2,1,0:T(1,128)S(1)}, u32[]{:S(2)}, u32[]{:S(2)}) collective-permute-start(f32[10,1,256]{2,1,0:T(1,128)S(1)} %get-tuple-element.99), channel_id=1, source_target_pairs={{2,0},{4,2},{6,4},{8,6},{10,8},{12,10},{14,12},{16,14},{18,16},{20... | collective-permute-start | bytes 30728 | tf_op jit(solution)/shard_map/ppermute | solution.py:20
  (130 other events, 2208.0 us)
where the time goes:
time: 654 us; the launch traced here: 650 us
  starting transfers between devices  358 us (55%)
  local copies, waits for them, and re-layouts  121 us (19%)
  waiting for transfers between devices  98.7 us (15%)
  other arithmetic  70.5 us (11%)
    ppermute x60, starting transfers between devices, padded_2(): lax.ppermute(head, axis, [((i + 1) % count, i) for i in range(ends)])  213 us
    ppermute x60, starting transfers between devices, padded_2(): lax.ppermute(tail, axis, [(i, (i + 1) % count) for i in range(ends)])  145 us
    ppermute x60, waiting for transfers between devices, padded_2(): lax.ppermute(tail, axis, [(i, (i + 1) % count) for i in range(ends)])  87.7 us
    reshape x1, local copies, waits for them, and re-layouts, coarsen(): coefficient.reshape(dims_now[0] // 2, 2, dims_now[1] // 2, 2, dims_now[2]...  68.4 us
    reduce_sum x2, other arithmetic, coarsen(): return jnp.mean(blocks, axis=(1, 3, 5))  26 us
    add x11, other arithmetic, chebyshev(): iterate = iterate + step_dir  17.4 us
  transfers between devices with their start and end apart: 120, of which 48 were waited for; matrix products, arithmetic and copies ran while one was open for 20% of the time, Pallas kernels for 0%

commit v1 on v0

v1 whole, which is shorter than its diff:
```python
import functools

import jax
import jax.numpy as jnp
from jax import lax
from jax.experimental import pallas as pl
from jax.experimental.pallas import tpu as pltpu
from jax.sharding import PartitionSpec as P

MESH = pl.DeviceIdType.MESH
F32 = jnp.float32
BF16 = jnp.bfloat16


def cheb_constants(sweeps, lower_edge, upper_edge):
    theta = 0.5 * (upper_edge + lower_edge)
    delta = 0.5 * (upper_edge - lower_edge)
    sigma = theta / delta
    rho = 1.0 / sigma
    steps = []
    for _ in range(1, sweeps):
        rho_next = 1.0 / (2.0 * sigma - rho)
        steps.append((rho_next * rho, 2.0 * rho_next / delta))
        rho = rho_next
    return theta, steps


THETA, ((MOM, GAIN),) = cheb_constants(2, 0.3, 2.0)
THETA_LOW, STEPS_LOW = cheb_constants(6, 0.05, 2.0)


def lanes(rows):
    return lax.broadcasted_iota(jnp.int32, (rows, 128), 1)


def roll_up(value):
    return pltpu.roll(value, 1, 1)


def roll_down(value):
    return pltpu.roll(value, 127, 1)


def operator_parts(centre, beside):
    faces = []
    diagonal = None
    for other in beside:
        face = jnp.where(other > 0.0, 0.5 * (centre + other), centre)
        diagonal = face if diagonal is None else diagonal + face
        faces.append(jnp.where(other > 0.0, face, 0.0))
    inside = centre > 0.0
    inverse = jnp.where(inside, 1.0 / diagonal, 0.0)
    diagonal = jnp.where(inside, diagonal, 0.0)
    return [face * inverse for face in faces], diagonal, inverse


def kernel(
    b_hbm, c_hbm, out_hbm,
    b_in, c_in, out_vm, perm,
    cF, bF, xF, x2F, dF, rF, gF, eC, e1, e2, pk, rpk,
    t1, t2, e3,
    c1, b1, x1L, x2L, x0L, xpL, dL, gL, stg, tL,
    c2, bd2, xa, xb, d2, inv2, g2, t3,
    local_sem, ss, rs,
):
    gx, gy, core = lax.axis_index("gx"), lax.axis_index("gy"), lax.axis_index("gz")
    nx, ny = lax.axis_size("gx"), lax.axis_size("gy")
    other = 1 - core
    sibling = (gx, gy, other)
    counter = [0]

    def peer(dx, dy):
        return (lax.rem(gx + dx + nx, nx), lax.rem(gy + dy + ny, ny), core)

    def send(src, dst, device):
        number = counter[0]
        counter[0] += 1
        copy = pltpu.make_async_remote_copy(
            src_ref=src, dst_ref=dst, send_sem=ss.at[number], recv_sem=rs.at[number],
            device_id=device, device_id_type=MESH,
        )
        copy.start()
        return copy

    load_c = pltpu.make_async_copy(c_hbm, c_in, local_sem.at[0])
    load_b = pltpu.make_async_copy(b_hbm, b_in, local_sem.at[1])
    load_c.start()
    load_b.start()

    for ref in (eC, e1, e2):

        @pl.loop(0, 22)
        def _(x, ref=ref):
            ref[x, core] = jnp.zeros((48, 128), F32)

    @pl.loop(0, 10)
    def _(x):
        e3[x, core] = jnp.zeros((16, 128), F32)

    @pl.loop(0, 3)
    def _(x):
        rF[x, :, 8:48, :] = jnp.zeros((4, 40, 128), F32)
        rF[x + 19, :, 8:48, :] = jnp.zeros((4, 40, 128), F32)

    peers14 = [(dx, dy) for dx in (-2, -1, 0, 1, 2) for dy in (-1, 0, 1) if (dx, dy) != (0, 0)]
    barrier = pltpu.get_barrier_semaphore()
    for dx, dy in peers14:
        pl.semaphore_signal(barrier, inc=1, device_id=peer(dx, dy), device_id_type=MESH)
    pl.semaphore_signal(barrier, inc=1, device_id=sibling, device_id_type=MESH)

    @pl.loop(0, 4)
    def _(j):
        z = lax.broadcasted_iota(jnp.int32, (128, 512), 0) + j * 128
        col = lax.broadcasted_iota(jnp.int32, (128, 512), 1)
        perm[pl.ds(pl.multiple_of(j * 128, 128), 128), :] = jnp.where(
            z == 4 * (col % 128) + col // 128, 1.0, 0.0
        ).astype(BF16)

    def spread(source, target):
        @pl.loop(0, 2)
        def _(half):
            rows = source[pl.ds(half * 8, 8)].reshape(256, 512)
            high = rows.astype(BF16)
            low = (rows - high.astype(F32)).astype(BF16)
            table = perm[...]
            result = jnp.dot(high, table, preferred_element_type=F32) + jnp.dot(
                low, table, preferred_element_type=F32
            )
            for k in range(4):
                target[pl.ds(half * 8 + 3, 8), k, 8:40, :] = result[
                    :, k * 128 : (k + 1) * 128
                ].reshape(8, 32, 128)

    load_c.wait()
    spread(c_in, cF)
    pl.semaphore_wait(barrier, len(peers14) + 1)
    face_c = [
        send(cF.at[3:6, :, 8:40], cF.at[19:22, :, 8:40], peer(-1, 0)),
        send(cF.at[16:19, :, 8:40], cF.at[0:3, :, 8:40], peer(1, 0)),
    ]
    load_b.wait()
    spread(b_in, bF)

    @pl.loop(0, 16)
    def _(x):
        for k in range(4):
            pk[0, x, k, 0:4, :] = cF[x + 3, k, 8:12, :]
            pk[0, x, k, 4:8, :] = bF[x + 3, k, 8:12, :]
            pk[1, x, k, 0:4, :] = cF[x + 3, k, 36:40, :]
            pk[1, x, k, 4:8, :] = bF[x + 3, k, 36:40, :]

    halo = [
        send(pk.at[0], rpk.at[1, 3:19], peer(0, -1)),
        send(pk.at[1], rpk.at[0, 3:19], peer(0, 1)),
        send(pk.at[0, 0:3], rpk.at[1, 19:22], peer(-1, -1)),
        send(pk.at[0, 13:16], rpk.at[1, 0:3], peer(1, -1)),
        send(pk.at[1, 0:3], rpk.at[0, 19:22], peer(-1, 1)),
        send(pk.at[1, 13:16], rpk.at[0, 0:3], peer(1, 1)),
    ]
    face_b = [
        send(bF.at[3:5, :, 8:40], bF.at[19:21, :, 8:40], peer(-1, 0)),
        send(bF.at[17:19, :, 8:40], bF.at[1:3, :, 8:40], peer(1, 0)),
    ]

    @pl.loop(0, 8)
    def _(i):
        for k in range(4):
            t1[0, k, 8:40, :] = cF[2 * i + 3, k, 8:40, :] + cF[2 * i + 4, k, 8:40, :]
        for q in range(2):
            total = None
            for k in (2 * q, 2 * q + 1):
                for start in (8, 9):
                    part = t1[0, k, pl.ds(start, 16, stride=2), :]
                    total = part if total is None else total + part
            c1[i + 6, q, core, 16:32, :] = total * (0.125 * 0.25)

    @pl.loop(0, 4)
    def _(i):
        total = None
        for q in range(2):
            tL[0, q, 0, 16:32, :] = c1[2 * i + 6, q, core, 16:32, :] + c1[2 * i + 7, q, core, 16:32, :]
            for start in (16, 17):
                part = tL[0, q, 0, pl.ds(start, 8, stride=2), :]
                total = part if total is None else total + part
        c2[i + 8, core, 16:24, :] = total * (0.125 * 0.25)

    rows_of = {0: (slice(16, 32), slice(16, 32)), -1: (slice(16, 24), slice(32, 40)), 1: (slice(24, 32), slice(8, 16))}
    planes_c1 = {0: (slice(6, 14), slice(6, 14)), -1: (slice(6, 12), slice(14, 20)), 1: (slice(8, 14), slice(0, 6))}
    halo_c1 = []
    for dx, dy in peers14:
        if abs(dx) < 2:
            (xs, xd), (ys, yd) = planes_c1[dx], rows_of[dy]
            halo_c1.append(send(c1.at[xs, :, core, ys], c1.at[xd, :, core, yd], peer(dx, dy)))
    halo_c2 = [
        send(
            c2.at[8:12, core, 16:24],
            c2.at[8 - 4 * dx : 12 - 4 * dx, core, 16 - 8 * dy : 24 - 8 * dy],
            peer(dx, dy),
        )
        for dx, dy in peers14
    ]

    for copy in face_c + halo:
        copy.wait_recv()

    @pl.loop(0, 22)
    def _(x):
        for k in range(4):
            cF[x, k, 4:8, :] = rpk[0, x, k, 0:4, :]
            bF[x, k, 4:8, :] = rpk[0, x, k, 4:8, :]
            cF[x, k, 40:44, :] = rpk[1, x, k, 0:4, :]
            bF[x, k, 40:44, :] = rpk[1, x, k, 4:8, :]

    def clear_planes(ref, first, count, condition):
        @pl.when(condition)
        def _():
            @pl.loop(first, first + count)
            def _(x):
                if ref.shape[1] == 4:
                    ref[x, :, 0:48, :] = jnp.zeros((4, 48, 128), F32)
                elif len(ref.shape) == 5:
                    for q in range(2):
                        ref[x, q, core] = jnp.zeros(ref.shape[3:], F32)
                else:
                    ref[x, core] = jnp.zeros(ref.shape[2:], F32)

    def clear_rows(ref, first, count, condition):
        zero = jnp.zeros((count, 128), F32)

        @pl.when(condition)
        def _():
            @pl.loop(0, ref.shape[0])
            def _(x):
                if ref.shape[1] == 4:
                    for k in range(4):
                        ref[x, k, first : first + count, :] = zero
                elif len(ref.shape) == 5:
                    for q in range(2):
                        ref[x, q, core, first : first + count, :] = zero
                else:
                    ref[x, core, first : first + count, :] = zero

    clear_planes(cF, 0, 3, gx == 0)
    clear_planes(cF, 19, 3, gx == nx - 1)
    clear_rows(cF, 4, 4, gy == 0)
    clear_rows(cF, 40, 4, gy == ny - 1)

    edge_phase = 3 * other

    def swap(source, target, first, last, rows):
        return send(
            source.at[first:last, edge_phase, rows], target.at[first:last, core, rows], sibling
        )

    CWIN, CUP, CDOWN = slice(4, 44), slice(3, 43), slice(5, 45)
    WIN, UP, DOWN = slice(8, 48), slice(7, 47), slice(9, 49)
    lane40 = lanes(40)

    def left_of(ref, edge, x, k, win):
        if k:
            return ref[x, k - 1, win, :]
        return roll_up(jnp.where(lane40 == 127, edge[x, 0, win, :], ref[x, 3, win, :]))

    def right_of(ref, edge, x, k, win):
        if k < 3:
            return ref[x, k + 1, win, :]
        return roll_down(jnp.where(lane40 == 0, edge[x, 1, win, :], ref[x, 0, win, :]))

    def planes(first, last, group, body):
        count = last - first

        @pl.loop(0, count // group)
        def _(j):
            for store_all in [body(first + j * group + u) for u in range(group)]:
                store_all()

        for store_all in [body(last - 1 - u) for u in range(count % group)]:
            store_all()

    INNER, OUTER = (1, 2), (0, 3)

    def setup_fine(phases):
        def body(x):
            results = []
            for k in phases:
                beside = [
                    cF[x - 1, k, CWIN, :], cF[x + 1, k, CWIN, :], cF[x, k, CUP, :], cF[x, k, CDOWN, :],
                    left_of(cF, eC, x, k, CWIN), right_of(cF, eC, x, k, CWIN),
                ]
                weights, diagonal, inverse = operator_parts(cF[x, k, CWIN, :], beside)
                results.append((k, weights, diagonal, bF[x, k, CWIN, :] * inverse * (1.0 / THETA)))

            def store_all():
                for k, weights, diagonal, iterate in results:
                    for n, weight in enumerate(weights):
                        gF[n, x - 1, k] = weight
                    dF[x, k] = diagonal
                    xF[x, k, WIN, :] = iterate

            return store_all

        planes(1, 21, 1, body)

    def sum_fine(ref, edge, x, k):
        return (
            gF[0, x - 1, k] * ref[x - 1, k, WIN, :]
            + gF[1, x - 1, k] * ref[x + 1, k, WIN, :]
            + gF[2, x - 1, k] * ref[x, k, UP, :]
            + gF[3, x - 1, k] * ref[x, k, DOWN, :]
            + gF[4, x - 1, k] * left_of(ref, edge, x, k, WIN)
            + gF[5, x - 1, k] * right_of(ref, edge, x, k, WIN)
        )

    def sweep_fine(target, source, edge, first, last, phases, formula):
        def body(x):
            results = [(k, formula(x, k, sum_fine(source, edge, x, k))) for k in phases]

            def store_all():
                for k, value in results:
                    target[x, k, WIN, :] = value

            return store_all

        planes(first, last, 2, body)

    first = 1.0 + MOM + GAIN * (THETA - 1.0)

    def pre_step(x, k, total):
        return first * xF[x, k, WIN, :] + GAIN * total

    def residual(x, k, total):
        return dF[x, k] * (THETA * xF[x, k, WIN, :] - x2F[x, k, WIN, :] + total)

    copy = swap(cF, eC, 1, 21, slice(0, 48))
    for other_copy in face_b:
        other_copy.wait_recv()
    for other_copy in face_b + halo + face_c:
        other_copy.wait_send()
    setup_fine(INNER)
    copy.wait()
    setup_fine(OUTER)
    copy = swap(xF, e1, 2, 20, WIN)
    sweep_fine(x2F, xF, e1, 2, 20, INNER, pre_step)
    copy.wait()
    sweep_fine(x2F, xF, e1, 2, 20, OUTER, pre_step)
    copy = swap(x2F, e2, 3, 19, WIN)
    far = [
        send(x2F.at[17:18, :, WIN], x2F.at[1:2, :, WIN], peer(1, 0)),
        send(x2F.at[4:5, :, WIN], x2F.at[20:21, :, WIN], peer(-1, 0)),
    ]
    sweep_fine(rF, x2F, e2, 3, 19, INNER, residual)
    copy.wait()
    sweep_fine(rF, x2F, e2, 3, 19, OUTER, residual)

    @pl.loop(0, 10)
    def _(i):
        for k in range(4):
            t1[i, k, WIN, :] = 0.125 * (
                rF[2 * i, k, WIN, :]
                + 3.0 * (rF[2 * i + 1, k, WIN, :] + rF[2 * i + 2, k, WIN, :])
                + rF[2 * i + 3, k, WIN, :]
            )
            part = [t1[i, k, pl.ds(s, 16, stride=2), :] for s in (11, 12, 13, 14)]
            t2[i, k] = 0.125 * (part[0] + 3.0 * (part[1] + part[2]) + part[3])

    copy = send(t2.at[:, edge_phase], e3.at[:, core], sibling)
    copy.wait()
    lane16 = lanes(16)

    @pl.loop(0, 10)
    def _(i):
        p = [t2[i, k] for k in range(4)]
        before = roll_up(jnp.where(lane16 == 127, e3[i, 0], p[3]))
        after = roll_down(jnp.where(lane16 == 0, e3[i, 1], p[0]))
        b1[i + 5, 0, core, 16:32, :] = 0.125 * (before + 3.0 * (p[0] + p[1]) + p[2])
        b1[i + 5, 1, core, 16:32, :] = 0.125 * (p[1] + 3.0 * (p[2] + p[3]) + after)

    halo_b1 = []
    for dx, dy in peers14:
        if abs(dx) < 2:
            ys, yd = rows_of[dy]
            if dx == 0:
                halo_b1.append(send(b1.at[5:15, :, core, ys], b1.at[5:15, :, core, yd], peer(dx, dy)))
            else:
                xs, xd, near, side = (
                    (slice(9, 13), slice(1, 5), slice(13, 15), 0)
                    if dx == 1
                    else (slice(7, 11), slice(15, 19), slice(5, 7), 1)
                )
                halo_b1.append(send(b1.at[near, :, core, ys], stg.at[side, :, :, yd], peer(dx, dy)))
                halo_b1.append(send(b1.at[xs, :, core, ys], b1.at[xd, :, core, yd], peer(dx, dy)))

    for copy in halo_c1 + halo_c2:
        copy.wait()
    clear_planes(c1, 0, 6, gx == 0)
    clear_planes(c1, 14, 6, gx == nx - 1)
    clear_rows(c1, 8, 8, gy == 0)
    clear_rows(c1, 32, 8, gy == ny - 1)
    clear_planes(c2, 4, 4, gx == 0)
    clear_planes(c2, 0, 4, gx <= 1)
    clear_planes(c2, 12, 4, gx == nx - 1)
    clear_planes(c2, 16, 4, gx >= nx - 2)
    clear_rows(c2, 8, 8, gy == 0)
    clear_rows(c2, 24, 8, gy == ny - 1)
    hand = [
        send(c1.at[:, :, core, 8:40], c1.at[:, :, core, 8:40], sibling),
        send(c2.at[:, core, 8:32], c2.at[:, core, 8:32], sibling),
    ]
    for copy in hand:
        copy.wait()

    lane32, lane24 = lanes(32), lanes(24)
    WL, UL, DL = slice(8, 40), slice(7, 39), slice(9, 41)
    W2, U2, D2 = slice(8, 32), slice(7, 31), slice(9, 33)

    def before_pair(halves, lane):
        turned = [roll_up(half) for half in halves]
        return [jnp.where(lane == 0, 0.0, turned[0]), jnp.where(lane == 0, turned[0], turned[1])]

    def after_pair(halves, lane):
        turned = [roll_down(half) for half in halves]
        return [jnp.where(lane == 127, turned[1], turned[0]), jnp.where(lane == 127, 0.0, turned[1])]

    def z_mid(ref, x):
        p0 = [ref[x, 0, t, WL, :] for t in range(2)]
        p1 = [ref[x, 1, t, WL, :] for t in range(2)]
        return [(before_pair(p1, lane32), p1), (p0, after_pair(p0, lane32))]

    @pl.loop(1, 19)
    def _(x):
        z_list = z_mid(c1, x)
        for q in range(2):
            for t in range(2):
                beside = [
                    c1[x - 1, q, t, WL, :], c1[x + 1, q, t, WL, :], c1[x, q, t, UL, :], c1[x, q, t, DL, :],
                    z_list[q][0][t], z_list[q][1][t],
                ]
                weights, diagonal, inverse = operator_parts(c1[x, q, t, WL, :], beside)
                for n, weight in enumerate(weights):
                    gL[n, x - 1, q, t] = weight
                dL[x, q, t] = diagonal
                x0L[x, q, t, WL, :] = inverse * (1.0 / THETA)

    @pl.loop(1, 19)
    def _(x):
        halves = [c2[x, t, W2, :] for t in range(2)]
        low, high = before_pair(halves, lane24), after_pair(halves, lane24)
        for t in range(2):
            beside = [
                c2[x - 1, t, W2, :], c2[x + 1, t, W2, :], c2[x, t, U2, :], c2[x, t, D2, :], low[t], high[t],
            ]
            weights, _, inverse = operator_parts(halves[t], beside)
            for n, weight in enumerate(weights):
                g2[n, x - 1, t] = weight
            inv2[x, t] = inverse

    for copy in halo_b1:
        copy.wait()
    for side, at in ((0, 5), (1, 13)):

        @pl.when((gx > 0) if side == 0 else (gx < nx - 1))
        def _(side=side, at=at):
            for n in range(2):
                for q in range(2):
                    b1[at + n, q, core, WL, :] = b1[at + n, q, core, WL, :] + stg[side, n, q, WL, :]

    @pl.loop(1, 19)
    def _(x):
        for q in range(2):
            x1L[x, q, core, WL, :] = b1[x, q, core, WL, :] * x0L[x, q, core, WL, :]

    copy = send(x1L.at[1:19, :, core, 8:40], x1L.at[1:19, :, core, 8:40], sibling)
    copy.wait()

    def sum_mid(ref, x):
        z_list = z_mid(ref, x)
        return {
            (q, t): gL[0, x - 1, q, t] * ref[x - 1, q, t, WL, :]
            + gL[1, x - 1, q, t] * ref[x + 1, q, t, WL, :]
            + gL[2, x - 1, q, t] * ref[x, q, t, UL, :]
            + gL[3, x - 1, q, t] * ref[x, q, t, DL, :]
            + gL[4, x - 1, q, t] * z_list[q][0][t]
            + gL[5, x - 1, q, t] * z_list[q][1][t]
            for q in range(2)
            for t in range(2)
        }

    def sweep_mid(target, source, first, last, formula):
        def body(x):
            results = {at: formula(x, *at, total) for at, total in sum_mid(source, x).items()}

            def store_all():
                for (q, t), value in results.items():
                    target[x, q, t, WL, :] = value

            return store_all

        planes(first, last, 2, body)

    sweep_mid(
        x2L, x1L, 2, 18, lambda x, q, t, total: first * x1L[x, q, t, WL, :] + GAIN * total
    )
    sweep_mid(
        xpL, x2L, 5, 15,
        lambda x, q, t, total: dL[x, q, t] * (THETA * x1L[x, q, t, WL, :] - x2L[x, q, t, WL, :] + total),
    )

    lane8 = lanes(8)

    @pl.loop(0, 4)
    def _(i):
        coarse = []
        for q in range(2):
            halves = []
            for t in range(2):
                tL[0, q, t, WL, :] = 0.125 * (
                    xpL[2 * i + 5, q, t, WL, :]
                    + 3.0 * (xpL[2 * i + 6, q, t, WL, :] + xpL[2 * i + 7, q, t, WL, :])
                    + xpL[2 * i + 8, q, t, WL, :]
                )
                part = [tL[0, q, t, pl.ds(s, 8, stride=2), :] for s in (15, 16, 17, 18)]
                halves.append(0.125 * (part[0] + 3.0 * (part[1] + part[2]) + part[3]))
            coarse.append(halves)
        low, high = before_pair(coarse[1], lane8), after_pair(coarse[0], lane8)
        pair = [0.125 * (low[t] + 3.0 * (coarse[0][t] + coarse[1][t]) + high[t]) for t in range(2)]
        mine = jnp.where(core == 0, pair[0], pair[1])
        bd2[i + 8, core, 16:24, :] = mine * inv2[i + 8, core, 8:16, :]

    halo_b2 = [
        send(
            bd2.at[8:12, core, 16:24],
            bd2.at[8 - 4 * dx : 12 - 4 * dx, core, 16 - 8 * dy : 24 - 8 * dy],
            peer(dx, dy),
        )
        for dx, dy in peers14
    ]
    for copy in halo_b2:
        copy.wait()
    copy = send(bd2.at[:, core, 8:32], bd2.at[:, core, 8:32], sibling)
    copy.wait()

    @pl.loop(0, 20)
    def _(x):
        for t in range(2):
            scaled = jnp.where(c2[x, t, W2, :] > 0.0, bd2[x, t, W2, :], 0.0)
            bd2[x, t, W2, :] = scaled
            d2[x, t] = scaled * (1.0 / THETA_LOW)
            xa[x, t, W2, :] = scaled * (1.0 / THETA_LOW)

    now, later = xa, xb
    for number, (mom, gain) in enumerate(STEPS_LOW):

        def body(x, now=now, later=later, mom=mom, gain=gain):
            halves = [now[x, t, W2, :] for t in range(2)]
            low, high = before_pair(halves, lane24), after_pair(halves, lane24)
            steps = []
            for t in range(2):
                total = (
                    g2[0, x - 1, t] * now[x - 1, t, W2, :]
                    + g2[1, x - 1, t] * now[x + 1, t, W2, :]
                    + g2[2, x - 1, t] * now[x, t, U2, :]
                    + g2[3, x - 1, t] * now[x, t, D2, :]
                    + g2[4, x - 1, t] * low[t]
                    + g2[5, x - 1, t] * high[t]
                )
                steps.append(mom * d2[x, t] + gain * (bd2[x, t, W2, :] - halves[t] + total))

            def store_all():
                for t in range(2):
                    d2[x, t] = steps[t]
                    later[x, t, W2, :] = halves[t] + steps[t]

            return store_all

        planes(number + 1, 19 - number, 4, body)
        now, later = later, now
    bottom = now

    @pl.loop(0, 8)
    def _(i):
        for odd in range(2):
            x = 2 * i + 2 + odd
            mixed = [
                0.75 * bottom[i + 6, t, W2, :] + 0.25 * bottom[i + 5 + 2 * odd, t, W2, :]
                for t in range(2)
            ]
            low, high = before_pair(mixed, lane24), after_pair(mixed, lane24)
            for q, side in ((0, low), (1, high)):
                for t in range(2):
                    t3[q, t, W2, :] = 0.75 * mixed[t] + 0.25 * side[t]
                    centre = 0.75 * t3[q, t, 12:28, :]
                    x0L[x, q, t, pl.ds(8, 16, stride=2), :] = centre + 0.25 * t3[q, t, 11:27, :]
                    x0L[x, q, t, pl.ds(9, 16, stride=2), :] = centre + 0.25 * t3[q, t, 13:29, :]
                    x0L[x, q, t, WL, :] = jnp.where(
                        c1[x, q, t, WL, :] > 0.0, x2L[x, q, t, WL, :] + x0L[x, q, t, WL, :], 0.0
                    )

    def post_first(x, q, t, total):
        start = x0L[x, q, t, WL, :]
        return start + (THETA * x1L[x, q, t, WL, :] - start + total) * (1.0 / THETA)

    def post_second(x, q, t, total):
        here = xpL[x, q, t, WL, :]
        return (
            here
            + MOM * (here - x0L[x, q, t, WL, :])
            + GAIN * (THETA * x1L[x, q, t, WL, :] - here + total)
        )

    sweep_mid(xpL, x0L, 3, 17, post_first)
    sweep_mid(x2L, xpL, 4, 16, post_second)

    for copy in far:
        copy.wait()
    has_left = jnp.where(core == 1, 1.0, 0.0)
    has_right = jnp.where(core == 0, 1.0, 0.0)

    @pl.loop(0, 10)
    def _(i):
        for odd in range(2):
            x = 2 * i + 1 + odd

            def mixed(q, t):
                return 0.75 * x2L[i + 5, q, t, WL, :] + 0.25 * x2L[i + 4 + 2 * odd, q, t, WL, :]

            m0, m1 = mixed(0, core), mixed(1, core)
            before = roll_up(jnp.where(lane32 == 127, has_left * mixed(1, other), m1))
            after = roll_down(jnp.where(lane32 == 0, has_right * mixed(0, other), m0))
            fine = [
                0.75 * m0 + 0.25 * before, 0.75 * m0 + 0.25 * m1,
                0.75 * m1 + 0.25 * m0, 0.75 * m1 + 0.25 * after,
            ]
            for k in range(4):
                tL[0, k // 2, k % 2, WL, :] = fine[k]
                centre = 0.75 * tL[0, k // 2, k % 2, 14:34, :]
                cF[x, k, pl.ds(8, 20, stride=2), :] = centre + 0.25 * tL[0, k // 2, k % 2, 13:33, :]
                cF[x, k, pl.ds(9, 20, stride=2), :] = centre + 0.25 * tL[0, k // 2, k % 2, 15:35, :]
                cF[x, k, WIN, :] = cF[x, k, WIN, :] + x2F[x, k, WIN, :]

    def last_first(x, k, total):
        start = cF[x, k, WIN, :]
        return start + (THETA * xF[x, k, WIN, :] - start + total) * (1.0 / THETA)

    def last_second(x, k, total):
        here = rF[x, k, WIN, :]
        return (
            here
            + MOM * (here - cF[x, k, WIN, :])
            + GAIN * (THETA * xF[x, k, WIN, :] - here + total)
        )

    copy = swap(cF, e1, 2, 20, WIN)
    sweep_fine(rF, cF, e1, 2, 20, INNER, last_first)
    copy.wait()
    sweep_fine(rF, cF, e1, 2, 20, OUTER, last_first)
    copy = swap(rF, e2, 3, 19, WIN)
    sweep_fine(x2F, rF, e2, 3, 19, INNER, last_second)
    copy.wait()
    sweep_fine(x2F, rF, e2, 3, 19, OUTER, last_second)

    @pl.loop(0, 2)
    def _(half):
        total = None
        for k in range(4):
            rows = x2F[pl.ds(half * 8 + 3, 8), k, 12:44, :].reshape(256, 128)
            high = rows.astype(BF16)
            low = (rows - high.astype(F32)).astype(BF16)
            table = perm[:, k * 128 : (k + 1) * 128]
            for part in (high, low):
                product = lax.dot_general(part, table, (((1,), (1,)), ((), ())), preferred_element_type=F32)
                total = product if total is None else total + product
        out_vm[pl.ds(half * 8, 8)] = total.reshape(8, 32, 512)

    store = pltpu.make_async_copy(out_vm, out_hbm, local_sem.at[2])
    store.start()
    store.wait()


def local(right_side, coefficient):
    def vmem(*shape):
        return pltpu.VMEM(shape, F32)

    inputs, fine, mid, low = (22, 4, 48, 128), (22, 4, 56, 128), (20, 2, 2, 48, 128), (20, 2, 40, 128)
    edge = (22, 2, 48, 128)
    scratch = [
        vmem(16, 32, 512), vmem(16, 32, 512), vmem(16, 32, 512), pltpu.VMEM((512, 512), BF16),
        vmem(*fine), vmem(*inputs), vmem(*fine), vmem(*fine), vmem(22, 4, 40, 128), vmem(*fine), vmem(6, 20, 4, 40, 128),
        vmem(*edge), vmem(*edge), vmem(*edge),
        vmem(2, 16, 4, 8, 128), vmem(2, 22, 4, 8, 128),
        vmem(10, 4, 48, 128), vmem(10, 4, 16, 128), vmem(10, 2, 16, 128),
        vmem(*mid), vmem(*mid), vmem(*mid), vmem(*mid), vmem(*mid), vmem(*mid), vmem(20, 2, 2, 32, 128),
        vmem(6, 18, 2, 2, 32, 128), vmem(2, 2, 2, 48, 128), vmem(1, 2, 2, 48, 128),
        vmem(*low), vmem(*low), vmem(*low), vmem(*low), vmem(20, 2, 24, 128), vmem(20, 2, 24, 128),
        vmem(6, 18, 2, 24, 128), vmem(2, 2, 40, 128),
        pltpu.SemaphoreType.DMA((3,)), pltpu.SemaphoreType.DMA((80,)), pltpu.SemaphoreType.DMA((80,)),
    ]
    return pl.pallas_call(
        kernel,
        out_shape=jax.ShapeDtypeStruct((16, 32, 512), F32),
        in_specs=[pl.BlockSpec(memory_space=pl.ANY)] * 2,
        out_specs=pl.BlockSpec(memory_space=pl.ANY),
        scratch_shapes=scratch,
        compiler_params=pltpu.CompilerParams(
            collective_id=0, has_side_effects=True, vmem_limit_bytes=63 * 2**20
        ),
    )(right_side, coefficient)


def solution(mesh):
    return jax.shard_map(
        local,
        mesh=mesh,
        in_specs=(P("gx", "gy", "gz"), P("gx", "gy", "gz")),
        out_specs=P("gx", "gy", "gz"),
        check_vma=False,
    )
```

time: 654 us -> 74.2 us (0.11)
  the two profiles are of different devices: /device:TPU:137 before, /device:TPU:1 now
where the time goes in v1:
time: 74.2 us; the launch traced here: 74 us
  Pallas kernels  71.7 us (97%)
  local copies, waits for them, and re-layouts  2.29 us (3%)
    pallas_call x1, Pallas kernels, local(): pl.pallas_call(kernel, out_shape=jax.ShapeDtypeStruct((16, 32, 512), F32)...  71.7 us
    unnamed x1, local copies, waits for them, and re-layouts  2.29 us

profile of v1, /device:TPU:1, one launch (start us, length us, event | category | flops | bytes accessed | tf_op | source)
XLA Modules:
  0.0 74.0 jit_solution(1149004523320726396)
XLA Ops:
  0.0 71.7 %shard_map.28 = f32[16,32,512]{2,1,0:T(8,128)} custom-call(f32[16,32,512]{2,1,0:T(8,128)} %b_hbm.1, f32[16,32,512]{2,1,0:T(8,128)} %c_hbm.1), custom_call_target="tpu_custom_call" | custom-call | tf_op jit(solution)/shard_map/pallas_call | solution.py:697
  71.7 2.3 %copy.4 = f32[16,32,512]{2,1,0:T(8,128)} copy(f32[16,32,512]{2,1,0:T(8,128)} %shard_map.28) | data formatting | bytes 2097152

commit v2 on v1

--- a/solution.py
+++ b/solution.py
@@ -56,8 +56,8 @@
 
 def kernel(
     b_hbm, c_hbm, out_hbm,
-    b_in, c_in, out_vm, perm,
-    cF, bF, xF, x2F, dF, rF, gF, eC, e1, e2, pk, rpk,
+    out_vm, b_in, c_in, perm,
+    cF, bF, xF, x2F, dF, rF, gF, eC, e1, e2, face_c_in, face_b_in, pk_out, pk_in, pk,
     t1, t2, e3,
     c1, b1, x1L, x2L, x0L, xpL, dL, gL, stg, tL,
     c2, bd2, xa, xb, d2, inv2, g2, t3,
@@ -82,31 +82,42 @@
         copy.start()
         return copy
 
+    peers14 = [(dx, dy) for dx in (-2, 2, -1, 1, 0) for dy in (-1, 1, 0) if (dx, dy) != (0, 0)]
+    peers8 = [(dx, dy) for dx, dy in peers14 if abs(dx) < 2]
+    barrier = pltpu.get_barrier_semaphore()
+    for dx, dy in peers8:
+        pl.semaphore_signal(barrier, inc=1, device_id=peer(dx, dy), device_id_type=MESH)
+    pl.semaphore_signal(barrier, inc=1, device_id=sibling, device_id_type=MESH)
     load_c = pltpu.make_async_copy(c_hbm, c_in, local_sem.at[0])
     load_b = pltpu.make_async_copy(b_hbm, b_in, local_sem.at[1])
     load_c.start()
     load_b.start()
-
-    for ref in (eC, e1, e2):
-
-        @pl.loop(0, 22)
-        def _(x, ref=ref):
-            ref[x, core] = jnp.zeros((48, 128), F32)
-
-    @pl.loop(0, 10)
+    pl.semaphore_wait(barrier, len(peers8) + 1)
+    face_c = [
+        send(c_hbm.at[0:3], face_c_in.at[1], peer(-1, 0)),
+        send(c_hbm.at[13:16], face_c_in.at[0], peer(1, 0)),
+    ]
+    face_b = [
+        send(b_hbm.at[0:2], face_b_in.at[1], peer(-1, 0)),
+        send(b_hbm.at[14:16], face_b_in.at[0], peer(1, 0)),
+    ]
+    load_c.wait()
+    load_b.wait()
+
+    @pl.loop(0, 16)
     def _(x):
-        e3[x, core] = jnp.zeros((16, 128), F32)
-
-    @pl.loop(0, 3)
-    def _(x):
-        rF[x, :, 8:48, :] = jnp.zeros((4, 40, 128), F32)
-        rF[x + 19, :, 8:48, :] = jnp.zeros((4, 40, 128), F32)
-
-    peers14 = [(dx, dy) for dx in (-2, -1, 0, 1, 2) for dy in (-1, 0, 1) if (dx, dy) != (0, 0)]
-    barrier = pltpu.get_barrier_semaphore()
-    for dx, dy in peers14:
-        pl.semaphore_signal(barrier, inc=1, device_id=peer(dx, dy), device_id_type=MESH)
-    pl.semaphore_signal(barrier, inc=1, device_id=sibling, device_id_type=MESH)
+        for side, rows in ((0, slice(0, 4)), (1, slice(28, 32))):
+            pk_out[side, x, 0:4, :] = c_in[x, rows, :]
+            pk_out[side, x, 4:8, :] = b_in[x, rows, :]
+
+    halo = [
+        send(pk_out.at[0], pk_in.at[1, 3:19], peer(0, -1)),
+        send(pk_out.at[1], pk_in.at[0, 3:19], peer(0, 1)),
+        send(pk_out.at[0, 0:3], pk_in.at[1, 19:22], peer(-1, -1)),
+        send(pk_out.at[0, 13:16], pk_in.at[1, 0:3], peer(1, -1)),
+        send(pk_out.at[1, 0:3], pk_in.at[0, 19:22], peer(-1, 1)),
+        send(pk_out.at[1, 13:16], pk_in.at[0, 0:3], peer(1, 1)),
+    ]
 
     @pl.loop(0, 4)
     def _(j):
@@ -116,51 +127,35 @@
             z == 4 * (col % 128) + col // 128, 1.0, 0.0
         ).astype(BF16)
 
-    def spread(source, target):
+    def spread(rows):
+        high = rows.astype(BF16)
+        low = (rows - high.astype(F32)).astype(BF16)
+        table = perm[...]
+        result = jnp.dot(high, table, preferred_element_type=F32) + jnp.dot(
+            low, table, preferred_element_type=F32
+        )
+        return [result[:, k * 128 : (k + 1) * 128] for k in range(4)]
+
+    for source, target in ((c_in, cF), (b_in, bF)):
+
         @pl.loop(0, 2)
-        def _(half):
-            rows = source[pl.ds(half * 8, 8)].reshape(256, 512)
-            high = rows.astype(BF16)
-            low = (rows - high.astype(F32)).astype(BF16)
-            table = perm[...]
-            result = jnp.dot(high, table, preferred_element_type=F32) + jnp.dot(
-                low, table, preferred_element_type=F32
-            )
-            for k in range(4):
-                target[pl.ds(half * 8 + 3, 8), k, 8:40, :] = result[
-                    :, k * 128 : (k + 1) * 128
-                ].reshape(8, 32, 128)
-
-    load_c.wait()
-    spread(c_in, cF)
-    pl.semaphore_wait(barrier, len(peers14) + 1)
-    face_c = [
-        send(cF.at[3:6, :, 8:40], cF.at[19:22, :, 8:40], peer(-1, 0)),
-        send(cF.at[16:19, :, 8:40], cF.at[0:3, :, 8:40], peer(1, 0)),
-    ]
-    load_b.wait()
-    spread(b_in, bF)
-
-    @pl.loop(0, 16)
+        def _(half, source=source, target=target):
+            for k, part in enumerate(spread(source[pl.ds(half * 8, 8)].reshape(256, 512))):
+                target[pl.ds(half * 8 + 3, 8), k, 8:40, :] = part.reshape(8, 32, 128)
+
+    @pl.loop(0, 22)
     def _(x):
-        for k in range(4):
-            pk[0, x, k, 0:4, :] = cF[x + 3, k, 8:12, :]
-            pk[0, x, k, 4:8, :] = bF[x + 3, k, 8:12, :]
-            pk[1, x, k, 0:4, :] = cF[x + 3, k, 36:40, :]
-            pk[1, x, k, 4:8, :] = bF[x + 3, k, 36:40, :]
-
-    halo = [
-        send(pk.at[0], rpk.at[1, 3:19], peer(0, -1)),
-        send(pk.at[1], rpk.at[0, 3:19], peer(0, 1)),
-        send(pk.at[0, 0:3], rpk.at[1, 19:22], peer(-1, -1)),
-        send(pk.at[0, 13:16], rpk.at[1, 0:3], peer(1, -1)),
-        send(pk.at[1, 0:3], rpk.at[0, 19:22], peer(-1, 1)),
-        send(pk.at[1, 13:16], rpk.at[0, 0:3], peer(1, 1)),
-    ]
-    face_b = [
-        send(bF.at[3:5, :, 8:40], bF.at[19:21, :, 8:40], peer(-1, 0)),
-        send(bF.at[17:19, :, 8:40], bF.at[1:3, :, 8:40], peer(1, 0)),
-    ]
+        for ref in (e1, e2):
+            ref[x, core] = jnp.zeros((48, 128), F32)
+
+    @pl.loop(0, 10)
+    def _(x):
+        e3[x, core] = jnp.zeros((16, 128), F32)
+
+    @pl.loop(0, 3)
+    def _(x):
+        rF[x, :, 8:48, :] = jnp.zeros((4, 40, 128), F32)
+        rF[x + 19, :, 8:48, :] = jnp.zeros((4, 40, 128), F32)
 
     @pl.loop(0, 8)
     def _(i):
@@ -172,44 +167,45 @@
                 for start in (8, 9):
                     part = t1[0, k, pl.ds(start, 16, stride=2), :]
                     total = part if total is None else total + part
-            c1[i + 6, q, core, 16:32, :] = total * (0.125 * 0.25)
+            c1[i + 4, q, core, 16:32, :] = total * (0.125 * 0.25)
 
     @pl.loop(0, 4)
     def _(i):
         total = None
         for q in range(2):
-            tL[0, q, 0, 16:32, :] = c1[2 * i + 6, q, core, 16:32, :] + c1[2 * i + 7, q, core, 16:32, :]
+            tL[0, q, 0, 16:32, :] = c1[2 * i + 4, q, core, 16:32, :] + c1[2 * i + 5, q, core, 16:32, :]
             for start in (16, 17):
                 part = tL[0, q, 0, pl.ds(start, 8, stride=2), :]
                 total = part if total is None else total + part
         c2[i + 8, core, 16:24, :] = total * (0.125 * 0.25)
 
-    rows_of = {0: (slice(16, 32), slice(16, 32)), -1: (slice(16, 24), slice(32, 40)), 1: (slice(24, 32), slice(8, 16))}
-    planes_c1 = {0: (slice(6, 14), slice(6, 14)), -1: (slice(6, 12), slice(14, 20)), 1: (slice(8, 14), slice(0, 6))}
-    halo_c1 = []
-    for dx, dy in peers14:
-        if abs(dx) < 2:
-            (xs, xd), (ys, yd) = planes_c1[dx], rows_of[dy]
-            halo_c1.append(send(c1.at[xs, :, core, ys], c1.at[xd, :, core, yd], peer(dx, dy)))
-    halo_c2 = [
-        send(
-            c2.at[8:12, core, 16:24],
-            c2.at[8 - 4 * dx : 12 - 4 * dx, core, 16 - 8 * dy : 24 - 8 * dy],
-            peer(dx, dy),
-        )
-        for dx, dy in peers14
-    ]
-
-    for copy in face_c + halo:
+    def spread_faces(arrived, target, depth, low, high):
+        for side, at in ((0, low), (1, high)):
+            for k, part in enumerate(spread(arrived[side].reshape(depth * 32, 512))):
+                target[at : at + depth, k, 8:40, :] = part.reshape(depth, 32, 128)
+
+    for copy in face_c:
         copy.wait_recv()
+    spread_faces(face_c_in, cF, 3, 0, 19)
+    for copy in face_b:
+        copy.wait_recv()
+    spread_faces(face_b_in, bF, 2, 1, 19)
+    for copy in halo:
+        copy.wait_recv()
+    for side in range(2):
+        for k, part in enumerate(spread(pk_in[side].reshape(176, 512))):
+            pk[side, :, k, :, :] = part.reshape(22, 8, 128)
+
+    CWIN, CUP, CDOWN = slice(4, 44), slice(3, 43), slice(5, 45)
+    WIN, UP, DOWN = slice(8, 48), slice(7, 47), slice(9, 49)
 
     @pl.loop(0, 22)
     def _(x):
         for k in range(4):
-            cF[x, k, 4:8, :] = rpk[0, x, k, 0:4, :]
-            bF[x, k, 4:8, :] = rpk[0, x, k, 4:8, :]
-            cF[x, k, 40:44, :] = rpk[1, x, k, 0:4, :]
-            bF[x, k, 40:44, :] = rpk[1, x, k, 4:8, :]
+            cF[x, k, 4:8, :] = pk[0, x, k, 0:4, :]
+            bF[x, k, 4:8, :] = pk[0, x, k, 4:8, :]
+            cF[x, k, 40:44, :] = pk[1, x, k, 0:4, :]
+            bF[x, k, 40:44, :] = pk[1, x, k, 4:8, :]
 
     def clear_planes(ref, first, count, condition):
         @pl.when(condition)
@@ -240,10 +236,26 @@
                 else:
                     ref[x, core, first : first + count, :] = zero
 
-    clear_planes(cF, 0, 3, gx == 0)
-    clear_planes(cF, 19, 3, gx == nx - 1)
-    clear_rows(cF, 4, 4, gy == 0)
-    clear_rows(cF, 40, 4, gy == ny - 1)
+    for ghost, cell, condition in ((2, 3, gx == 0), (19, 18, gx == nx - 1)):
+
+        @pl.when(condition)
+        def _(ghost=ghost, cell=cell):
+            cF[ghost] = cF[cell]
+
+    for ghost, cell, condition in ((7, 8, gy == 0), (40, 39, gy == ny - 1)):
+
+        @pl.when(condition)
+        def _(ghost=ghost, cell=cell):
+            @pl.loop(0, 22)
+            def _(x):
+                for k in range(4):
+                    cF[x, k, ghost : ghost + 1, :] = cF[x, k, cell : cell + 1, :]
+
+    @pl.loop(1, 21)
+    def _(x):
+        low = roll_down(cF[x, 0, CWIN, :])
+        high = roll_up(cF[x, 3, CWIN, :])
+        eC[x, core, CWIN, :] = jnp.where(core == 0, low, high)
 
     edge_phase = 3 * other
 
@@ -252,8 +264,6 @@
             source.at[first:last, edge_phase, rows], target.at[first:last, core, rows], sibling
         )
 
-    CWIN, CUP, CDOWN = slice(4, 44), slice(3, 43), slice(5, 45)
-    WIN, UP, DOWN = slice(8, 48), slice(7, 47), slice(9, 49)
     lane40 = lanes(40)
 
     def left_of(ref, edge, x, k, win):
@@ -287,8 +297,12 @@
                     cF[x - 1, k, CWIN, :], cF[x + 1, k, CWIN, :], cF[x, k, CUP, :], cF[x, k, CDOWN, :],
                     left_of(cF, eC, x, k, CWIN), right_of(cF, eC, x, k, CWIN),
                 ]
-                weights, diagonal, inverse = operator_parts(cF[x, k, CWIN, :], beside)
-                results.append((k, weights, diagonal, bF[x, k, CWIN, :] * inverse * (1.0 / THETA)))
+                centre = cF[x, k, CWIN, :]
+                pairs = [centre + value for value in beside]
+                twice = ((pairs[0] + pairs[1]) + (pairs[2] + pairs[3])) + (pairs[4] + pairs[5])
+                inverse = 1.0 / twice
+                weights = [pair * inverse for pair in pairs]
+                results.append((k, weights, 0.5 * twice, bF[x, k, CWIN, :] * inverse * (2.0 / THETA)))
 
             def store_all():
                 for k, weights, diagonal, iterate in results:
@@ -299,7 +313,7 @@
 
             return store_all
 
-        planes(1, 21, 1, body)
+        planes(1, 21, 2, body)
 
     def sum_fine(ref, edge, x, k):
         return (
@@ -321,7 +335,7 @@
 
             return store_all
 
-        planes(first, last, 2, body)
+        planes(first, last, 3, body)
 
     first = 1.0 + MOM + GAIN * (THETA - 1.0)
 
@@ -332,36 +346,88 @@
         return dF[x, k] * (THETA * xF[x, k, WIN, :] - x2F[x, k, WIN, :] + total)
 
     copy = swap(cF, eC, 1, 21, slice(0, 48))
-    for other_copy in face_b:
-        other_copy.wait_recv()
-    for other_copy in face_b + halo + face_c:
-        other_copy.wait_send()
+    rows_of = {0: (slice(16, 32), slice(16, 32)), -1: (slice(16, 24), slice(32, 40)), 1: (slice(24, 32), slice(8, 16))}
+    planes_c1 = {0: (slice(4, 12), slice(4, 12)), -1: (slice(4, 8), slice(12, 16)), 1: (slice(8, 12), slice(0, 4))}
+    halo_c1 = []
+    for dx, dy in peers8:
+        (xs, xd), (ys, yd) = planes_c1[dx], rows_of[dy]
+        halo_c1.append(send(c1.at[xs, :, core, ys], c1.at[xd, :, core, yd], peer(dx, dy)))
+    halo_c2 = [
+        send(
+            c2.at[8:12, core, 16:24],
+            c2.at[8 - 4 * dx : 12 - 4 * dx, core, 16 - 8 * dy : 24 - 8 * dy],
+            peer(dx, dy),
+        )
+        for dx, dy in peers14
+    ]
+
     setup_fine(INNER)
     copy.wait()
     setup_fine(OUTER)
+    for n, plane, condition in ((0, 2, gx == 0), (1, 17, gx == nx - 1)):
+
+        @pl.when(condition)
+        def _(n=n, plane=plane):
+            gF[n, plane] = jnp.zeros((4, 40, 128), F32)
+
+    for n, row, condition in ((2, 4, gy == 0), (3, 35, gy == ny - 1)):
+
+        @pl.when(condition)
+        def _(n=n, row=row):
+            @pl.loop(1, 19)
+            def _(x):
+                for k in range(4):
+                    gF[n, x, k, row : row + 1, :] = jnp.zeros((1, 128), F32)
+
     copy = swap(xF, e1, 2, 20, WIN)
     sweep_fine(x2F, xF, e1, 2, 20, INNER, pre_step)
     copy.wait()
     sweep_fine(x2F, xF, e1, 2, 20, OUTER, pre_step)
     copy = swap(x2F, e2, 3, 19, WIN)
-    far = [
-        send(x2F.at[17:18, :, WIN], x2F.at[1:2, :, WIN], peer(1, 0)),
-        send(x2F.at[4:5, :, WIN], x2F.at[20:21, :, WIN], peer(-1, 0)),
-    ]
     sweep_fine(rF, x2F, e2, 3, 19, INNER, residual)
     copy.wait()
     sweep_fine(rF, x2F, e2, 3, 19, OUTER, residual)
 
-    @pl.loop(0, 10)
-    def _(i):
-        for k in range(4):
-            t1[i, k, WIN, :] = 0.125 * (
+    for row, condition in ((8, gy == 0), (44, gy == ny - 1)):
+
+        @pl.when(condition)
+        def _(row=row):
+            @pl.loop(3, 19)
+            def _(x):
+                for k in range(4):
+                    rF[x, k, row : row + 4, :] = jnp.zeros((4, 128), F32)
+
+    def restrict_x(i):
+        results = [
+            0.125
+            * (
                 rF[2 * i, k, WIN, :]
                 + 3.0 * (rF[2 * i + 1, k, WIN, :] + rF[2 * i + 2, k, WIN, :])
                 + rF[2 * i + 3, k, WIN, :]
             )
+            for k in range(4)
+        ]
+
+        def store_all():
+            for k in range(4):
+                t1[i, k, WIN, :] = results[k]
+
+        return store_all
+
+    def restrict_y(i):
+        results = []
+        for k in range(4):
             part = [t1[i, k, pl.ds(s, 16, stride=2), :] for s in (11, 12, 13, 14)]
-            t2[i, k] = 0.125 * (part[0] + 3.0 * (part[1] + part[2]) + part[3])
+            results.append(0.125 * (part[0] + 3.0 * (part[1] + part[2]) + part[3]))
+
+        def store_all():
+            for k in range(4):
+                t2[i, k] = results[k]
+
+        return store_all
+
+    planes(0, 10, 2, restrict_x)
+    planes(0, 10, 2, restrict_y)
 
     copy = send(t2.at[:, edge_phase], e3.at[:, core], sibling)
     copy.wait()
@@ -372,28 +438,34 @@
         p = [t2[i, k] for k in range(4)]
         before = roll_up(jnp.where(lane16 == 127, e3[i, 0], p[3]))
         after = roll_down(jnp.where(lane16 == 0, e3[i, 1], p[0]))
-        b1[i + 5, 0, core, 16:32, :] = 0.125 * (before + 3.0 * (p[0] + p[1]) + p[2])
-        b1[i + 5, 1, core, 16:32, :] = 0.125 * (p[1] + 3.0 * (p[2] + p[3]) + after)
+        b1[i + 3, 0, core, 16:32, :] = 0.125 * (before + 3.0 * (p[0] + p[1]) + p[2])
+        b1[i + 3, 1, core, 16:32, :] = 0.125 * (p[1] + 3.0 * (p[2] + p[3]) + after)
 
     halo_b1 = []
-    for dx, dy in peers14:
-        if abs(dx) < 2:
-            ys, yd = rows_of[dy]
-            if dx == 0:
-                halo_b1.append(send(b1.at[5:15, :, core, ys], b1.at[5:15, :, core, yd], peer(dx, dy)))
-            else:
-                xs, xd, near, side = (
-                    (slice(9, 13), slice(1, 5), slice(13, 15), 0)
-                    if dx == 1
-                    else (slice(7, 11), slice(15, 19), slice(5, 7), 1)
-                )
-                halo_b1.append(send(b1.at[near, :, core, ys], stg.at[side, :, :, yd], peer(dx, dy)))
-                halo_b1.append(send(b1.at[xs, :, core, ys], b1.at[xd, :, core, yd], peer(dx, dy)))
-
+    for dx, dy in peers8:
+        ys, yd = rows_of[dy]
+        if dx == 0:
+            halo_b1.append(send(b1.at[3:13, :, core, ys], b1.at[3:13, :, core, yd], peer(dx, dy)))
+        else:
+            xs, xd, near, side = (
+                (slice(9, 11), slice(1, 3), slice(11, 13), 0)
+                if dx == 1
+                else (slice(5, 7), slice(13, 15), slice(3, 5), 1)
+            )
+            halo_b1.append(send(b1.at[near, :, core, ys], stg.at[side, :, :, yd], peer(dx, dy)))
+            halo_b1.append(send(b1.at[xs, :, core, ys], b1.at[xd, :, core, yd], peer(dx, dy)))
+
+    far = [
+        send(x2F.at[17:18, :, WIN], x2F.at[1:2, :, WIN], peer(1, 0)),
+        send(x2F.at[4:5, :, WIN], x2F.at[20:21, :, WIN], peer(-1, 0)),
+    ]
+
+    for copy in face_c + face_b + halo:
+        copy.wait_send()
     for copy in halo_c1 + halo_c2:
         copy.wait()
-    clear_planes(c1, 0, 6, gx == 0)
-    clear_planes(c1, 14, 6, gx == nx - 1)
+    clear_planes(c1, 0, 4, gx == 0)
+    clear_planes(c1, 12, 4, gx == nx - 1)
     clear_rows(c1, 8, 8, gy == 0)
     clear_rows(c1, 32, 8, gy == ny - 1)
     clear_planes(c2, 4, 4, gx == 0)
@@ -426,7 +498,7 @@
         p1 = [ref[x, 1, t, WL, :] for t in range(2)]
         return [(before_pair(p1, lane32), p1), (p0, after_pair(p0, lane32))]
 
-    @pl.loop(1, 19)
+    @pl.loop(1, 15)
     def _(x):
         z_list = z_mid(c1, x)
         for q in range(2):
@@ -441,22 +513,38 @@
                 dL[x, q, t] = diagonal
                 x0L[x, q, t, WL, :] = inverse * (1.0 / THETA)
 
-    @pl.loop(1, 19)
-    def _(x):
-        halves = [c2[x, t, W2, :] for t in range(2)]
-        low, high = before_pair(halves, lane24), after_pair(halves, lane24)
-        for t in range(2):
-            beside = [
-                c2[x - 1, t, W2, :], c2[x + 1, t, W2, :], c2[x, t, U2, :], c2[x, t, D2, :], low[t], high[t],
-            ]
-            weights, _, inverse = operator_parts(halves[t], beside)
-            for n, weight in enumerate(weights):
-                g2[n, x - 1, t] = weight
-            inv2[x, t] = inverse
-
-    for copy in halo_b1:
-        copy.wait()
-    for side, at in ((0, 5), (1, 13)):
+    def setup_low(first, last):
+        @pl.loop(first, last)
+        def _(x):
+            halves = [c2[x, t, W2, :] for t in range(2)]
+            low, high = before_pair(halves, lane24), after_pair(halves, lane24)
+            for t in range(2):
+                beside = [
+                    c2[x - 1, t, W2, :], c2[x + 1, t, W2, :], c2[x, t, U2, :], c2[x, t, D2, :], low[t], high[t],
+                ]
+                weights, _, inverse = operator_parts(halves[t], beside)
+                for n, weight in enumerate(weights):
+                    g2[n, x - 1, t] = weight
+                inv2[x, t] = inverse
+
+    setup_low(8, 12)
+
+    def scale_mid(first, last):
+        @pl.loop(first, last)
+        def _(x):
+            for q in range(2):
+                x1L[x, q, core, WL, :] = b1[x, q, core, WL, :] * x0L[x, q, core, WL, :]
+
+        return send(
+            x1L.at[first:last, :, core, 8:40], x1L.at[first:last, :, core, 8:40], sibling
+        )
+
+    for copy in halo_b1[-2:]:
+        copy.wait()
+    handed = [scale_mid(5, 11)]
+    for copy in halo_b1[:-2]:
+        copy.wait()
+    for side, at in ((0, 3), (1, 11)):
 
         @pl.when((gx > 0) if side == 0 else (gx < nx - 1))
         def _(side=side, at=at):
@@ -464,13 +552,9 @@
                 for q in range(2):
                     b1[at + n, q, core, WL, :] = b1[at + n, q, core, WL, :] + stg[side, n, q, WL, :]
 
-    @pl.loop(1, 19)
-    def _(x):
-        for q in range(2):
-            x1L[x, q, core, WL, :] = b1[x, q, core, WL, :] * x0L[x, q, core, WL, :]
-
-    copy = send(x1L.at[1:19, :, core, 8:40], x1L.at[1:19, :, core, 8:40], sibling)
-    copy.wait()
+    handed += [scale_mid(1, 5), scale_mid(11, 15)]
+    for copy in handed:
+        copy.wait()
 
     def sum_mid(ref, x):
         z_list = z_mid(ref, x)
@@ -498,10 +582,10 @@
         planes(first, last, 2, body)
 
     sweep_mid(
-        x2L, x1L, 2, 18, lambda x, q, t, total: first * x1L[x, q, t, WL, :] + GAIN * total
+        x2L, x1L, 2, 14, lambda x, q, t, total: first * x1L[x, q, t, WL, :] + GAIN * total
     )
     sweep_mid(
-        xpL, x2L, 5, 15,
+        xpL, x2L, 3, 13,
         lambda x, q, t, total: dL[x, q, t] * (THETA * x1L[x, q, t, WL, :] - x2L[x, q, t, WL, :] + total),
     )
 
@@ -514,9 +598,9 @@
             halves = []
             for t in range(2):
                 tL[0, q, t, WL, :] = 0.125 * (
-                    xpL[2 * i + 5, q, t, WL, :]
-                    + 3.0 * (xpL[2 * i + 6, q, t, WL, :] + xpL[2 * i + 7, q, t, WL, :])
-                    + xpL[2 * i + 8, q, t, WL, :]
+                    xpL[2 * i + 3, q, t, WL, :]
+                    + 3.0 * (xpL[2 * i + 4, q, t, WL, :] + xpL[2 * i + 5, q, t, WL, :])
+                    + xpL[2 * i + 6, q, t, WL, :]
                 )
                 part = [tL[0, q, t, pl.ds(s, 8, stride=2), :] for s in (15, 16, 17, 18)]
                 halves.append(0.125 * (part[0] + 3.0 * (part[1] + part[2]) + part[3]))
@@ -534,10 +618,22 @@
         )
         for dx, dy in peers14
     ]
-    for copy in halo_b2:
-        copy.wait()
-    copy = send(bd2.at[:, core, 8:32], bd2.at[:, core, 8:32], sibling)
-    copy.wait()
+    far_mid = [
+        send(x2L.at[8:10, :, :, 8:40], x2L.at[0:2, :, :, 8:40], peer(1, 0)),
+        send(x2L.at[6:8, :, :, 8:40], x2L.at[14:16, :, :, 8:40], peer(-1, 0)),
+    ]
+    setup_low(1, 8)
+    setup_low(12, 19)
+    handed = []
+    for group in (0, 1, 2):
+        for (dx, dy), copy in zip(peers14, halo_b2):
+            if abs(dx) == group:
+                copy.wait()
+        for at in sorted({8 - 4 * group, 8 + 4 * group}):
+            block = bd2.at[at : at + 4, core, 8:32]
+            handed.append(send(block, block, sibling))
+    for copy in handed:
+        copy.wait()
 
     @pl.loop(0, 20)
     def _(x):
@@ -576,10 +672,13 @@
         now, later = later, now
     bottom = now
 
+    for copy in far_mid:
+        copy.wait()
+
     @pl.loop(0, 8)
     def _(i):
         for odd in range(2):
-            x = 2 * i + 2 + odd
+            x = 2 * i + odd
             mixed = [
                 0.75 * bottom[i + 6, t, W2, :] + 0.25 * bottom[i + 5 + 2 * odd, t, W2, :]
                 for t in range(2)
@@ -587,10 +686,10 @@
             low, high = before_pair(mixed, lane24), after_pair(mixed, lane24)
             for q, side in ((0, low), (1, high)):
                 for t in range(2):
-                    t3[q, t, W2, :] = 0.75 * mixed[t] + 0.25 * side[t]
-                    centre = 0.75 * t3[q, t, 12:28, :]
-                    x0L[x, q, t, pl.ds(8, 16, stride=2), :] = centre + 0.25 * t3[q, t, 11:27, :]
-                    x0L[x, q, t, pl.ds(9, 16, stride=2), :] = centre + 0.25 * t3[q, t, 13:29, :]
+                    t3[odd, q, t, W2, :] = 0.75 * mixed[t] + 0.25 * side[t]
+                    centre = 0.75 * t3[odd, q, t, 12:28, :]
+                    x0L[x, q, t, pl.ds(8, 16, stride=2), :] = centre + 0.25 * t3[odd, q, t, 11:27, :]
+                    x0L[x, q, t, pl.ds(9, 16, stride=2), :] = centre + 0.25 * t3[odd, q, t, 13:29, :]
                     x0L[x, q, t, WL, :] = jnp.where(
                         c1[x, q, t, WL, :] > 0.0, x2L[x, q, t, WL, :] + x0L[x, q, t, WL, :], 0.0
                     )
@@ -607,8 +706,8 @@
             + GAIN * (THETA * x1L[x, q, t, WL, :] - here + total)
         )
 
-    sweep_mid(xpL, x0L, 3, 17, post_first)
-    sweep_mid(x2L, xpL, 4, 16, post_second)
+    sweep_mid(xpL, x0L, 1, 15, post_first)
+    sweep_mid(x2L, xpL, 2, 14, post_second)
 
     for copy in far:
         copy.wait()
@@ -621,7 +720,7 @@
             x = 2 * i + 1 + odd
 
             def mixed(q, t):
-                return 0.75 * x2L[i + 5, q, t, WL, :] + 0.25 * x2L[i + 4 + 2 * odd, q, t, WL, :]
+                return 0.75 * x2L[i + 3, q, t, WL, :] + 0.25 * x2L[i + 2 + 2 * odd, q, t, WL, :]
 
             m0, m1 = mixed(0, core), mixed(1, core)
             before = roll_up(jnp.where(lane32 == 127, has_left * mixed(1, other), m1))
@@ -631,10 +730,10 @@
                 0.75 * m1 + 0.25 * m0, 0.75 * m1 + 0.25 * after,
             ]
             for k in range(4):
-                tL[0, k // 2, k % 2, WL, :] = fine[k]
-                centre = 0.75 * tL[0, k // 2, k % 2, 14:34, :]
-                cF[x, k, pl.ds(8, 20, stride=2), :] = centre + 0.25 * tL[0, k // 2, k % 2, 13:33, :]
-                cF[x, k, pl.ds(9, 20, stride=2), :] = centre + 0.25 * tL[0, k // 2, k % 2, 15:35, :]
+                tL[odd, k // 2, k % 2, WL, :] = fine[k]
+                centre = 0.75 * tL[odd, k // 2, k % 2, 14:34, :]
+                cF[x, k, pl.ds(8, 20, stride=2), :] = centre + 0.25 * tL[odd, k // 2, k % 2, 13:33, :]
+                cF[x, k, pl.ds(9, 20, stride=2), :] = centre + 0.25 * tL[odd, k // 2, k % 2, 15:35, :]
                 cF[x, k, WIN, :] = cF[x, k, WIN, :] + x2F[x, k, WIN, :]
 
     def last_first(x, k, total):
@@ -658,43 +757,60 @@
     copy.wait()
     sweep_fine(x2F, rF, e2, 3, 19, OUTER, last_second)
 
-    @pl.loop(0, 2)
-    def _(half):
+    def store(part):
+        planes_of = pl.ds(part * 4, 4)
+        return pltpu.make_async_copy(out_vm.at[planes_of], out_hbm.at[planes_of], local_sem.at[2 + part])
+
+    for part in range(4):
         total = None
         for k in range(4):
-            rows = x2F[pl.ds(half * 8 + 3, 8), k, 12:44, :].reshape(256, 128)
+            rows = x2F[part * 4 + 3 : part * 4 + 7, k, 12:44, :].reshape(128, 128)
             high = rows.astype(BF16)
             low = (rows - high.astype(F32)).astype(BF16)
             table = perm[:, k * 128 : (k + 1) * 128]
-            for part in (high, low):
-                product = lax.dot_general(part, table, (((1,), (1,)), ((), ())), preferred_element_type=F32)
+            for piece in (high, low):
+                product = lax.dot_general(piece, table, (((1,), (1,)), ((), ())), preferred_element_type=F32)
                 total = product if total is None else total + product
-        out_vm[pl.ds(half * 8, 8)] = total.reshape(8, 32, 512)
-
-    store = pltpu.make_async_copy(out_vm, out_hbm, local_sem.at[2])
-    store.start()
-    store.wait()
+        out_vm[part * 4 : part * 4 + 4] = total.reshape(4, 32, 512)
+        store(part).start()
+    for part in range(4):
+        store(part).wait()
+
+
+def copy_kernel(source, target, buffer, read_sem, write_sem):
+    reads, writes = [], []
+    for n in range(8):
+        part = pl.ds(2 * n, 2)
+        reads.append(pltpu.make_async_copy(source.at[part], buffer.at[part], read_sem.at[n]))
+        writes.append(pltpu.make_async_copy(buffer.at[part], target.at[part], write_sem.at[n]))
+    for copy in reads:
+        copy.start()
+    for copy, after in zip(reads, writes):
+        copy.wait()
+        after.start()
+    for copy in writes:
+        copy.wait()
 
 
 def local(right_side, coefficient):
     def vmem(*shape):
         return pltpu.VMEM(shape, F32)
 
-    inputs, fine, mid, low = (22, 4, 48, 128), (22, 4, 56, 128), (20, 2, 2, 48, 128), (20, 2, 40, 128)
+    inputs, fine, mid, low = (22, 4, 48, 128), (22, 4, 56, 128), (16, 2, 2, 48, 128), (20, 2, 40, 128)
     edge = (22, 2, 48, 128)
     scratch = [
         vmem(16, 32, 512), vmem(16, 32, 512), vmem(16, 32, 512), pltpu.VMEM((512, 512), BF16),
         vmem(*fine), vmem(*inputs), vmem(*fine), vmem(*fine), vmem(22, 4, 40, 128), vmem(*fine), vmem(6, 20, 4, 40, 128),
         vmem(*edge), vmem(*edge), vmem(*edge),
-        vmem(2, 16, 4, 8, 128), vmem(2, 22, 4, 8, 128),
+        vmem(2, 3, 32, 512), vmem(2, 2, 32, 512), vmem(2, 16, 8, 512), vmem(2, 22, 8, 512), vmem(2, 22, 4, 8, 128),
         vmem(10, 4, 48, 128), vmem(10, 4, 16, 128), vmem(10, 2, 16, 128),
-        vmem(*mid), vmem(*mid), vmem(*mid), vmem(*mid), vmem(*mid), vmem(*mid), vmem(20, 2, 2, 32, 128),
-        vmem(6, 18, 2, 2, 32, 128), vmem(2, 2, 2, 48, 128), vmem(1, 2, 2, 48, 128),
+        vmem(*mid), vmem(*mid), vmem(*mid), vmem(*mid), vmem(*mid), vmem(*mid), vmem(16, 2, 2, 32, 128),
+        vmem(6, 14, 2, 2, 32, 128), vmem(2, 2, 2, 48, 128), vmem(2, 2, 2, 48, 128),
         vmem(*low), vmem(*low), vmem(*low), vmem(*low), vmem(20, 2, 24, 128), vmem(20, 2, 24, 128),
-        vmem(6, 18, 2, 24, 128), vmem(2, 2, 40, 128),
-        pltpu.SemaphoreType.DMA((3,)), pltpu.SemaphoreType.DMA((80,)), pltpu.SemaphoreType.DMA((80,)),
+        vmem(6, 18, 2, 24, 128), vmem(2, 2, 2, 40, 128),
+        pltpu.SemaphoreType.DMA((6,)), pltpu.SemaphoreType.DMA((80,)), pltpu.SemaphoreType.DMA((80,)),
     ]
-    return pl.pallas_call(
+    result = pl.pallas_call(
         kernel,
         out_shape=jax.ShapeDtypeStruct((16, 32, 512), F32),
         in_specs=[pl.BlockSpec(memory_space=pl.ANY)] * 2,
@@ -704,6 +820,13 @@
             collective_id=0, has_side_effects=True, vmem_limit_bytes=63 * 2**20
         ),
     )(right_side, coefficient)
+    return pl.pallas_call(
+        copy_kernel,
+        out_shape=jax.ShapeDtypeStruct((16, 32, 512), F32),
+        in_specs=[pl.BlockSpec(memory_space=pl.ANY)],
+        out_specs=pl.BlockSpec(memory_space=pl.ANY),
+        scratch_shapes=[vmem(16, 32, 512), pltpu.SemaphoreType.DMA((8,)), pltpu.SemaphoreType.DMA((8,))],
+    )(result)
 
 
 def solution(mesh):

time: 74.2 us -> 70.1 us (0.945)
  local copies, waits for them, and re-layouts: 2.29 us -> 0 us
  Pallas kernels: 71.7 us -> 70 us
    pallas_call x1, Pallas kernels: 71.7 us -> 67.9 us  [local(): pl.pallas_call(kernel, out_shape=jax.ShapeDtypeStruct((16, 32, 512), F32)...]
    unnamed x1 -> x0, local copies, waits for them, and re-layouts: 2.29 us -> none
    pallas_call x0 -> x1, Pallas kernels: none -> 2.09 us  [local(): pl.pallas_call(copy_kernel, out_shape=jax.ShapeDtypeStruct((16, 32, 512),...]
where the time goes in v2:
time: 70.1 us; the launch traced here: 70 us
  Pallas kernels  70 us (100%)
    pallas_call x1, Pallas kernels, local(): pl.pallas_call(kernel, out_shape=jax.ShapeDtypeStruct((16, 32, 512), F32)...  67.9 us
    pallas_call x1, Pallas kernels, local(): pl.pallas_call(copy_kernel, out_shape=jax.ShapeDtypeStruct((16, 32, 512),...  2.09 us

profile of v2, /device:TPU:1, one launch (start us, length us, event | category | flops | bytes accessed | tf_op | source)
XLA Modules:
  0.0 70.0 jit_solution(6085544912571522977)
XLA Ops:
  0.0 67.9 %shard_map.28.source = f32[16,32,512]{2,1,0:T(8,128)} custom-call(f32[16,32,512]{2,1,0:T(8,128)} %b_hbm.1, f32[16,32,512]{2,1,0:T(8,128)} %c_hbm.1), custom_call_target="tpu_custom_call" | custom-call | tf_op jit(solution)/shard_map/pallas_call | solution.py:813
  67.9 2.1 %shard_map.29 = f32[16,32,512]{2,1,0:T(8,128)} custom-call(f32[16,32,512]{2,1,0:T(8,128)} %shard_map.28.source), custom_call_target="tpu_custom_call" | custom-call | tf_op jit(solution)/shard_map/pallas_call | solution.py:823

commit v3 on v2

--- a/solution.py
+++ b/solution.py
@@ -313,7 +313,7 @@
 
             return store_all
 
-        planes(1, 21, 2, body)
+        planes(1, 21, 4 // len(phases), body)
 
     def sum_fine(ref, edge, x, k):
         return (
@@ -335,7 +335,23 @@
 
             return store_all
 
-        planes(first, last, 3, body)
+        planes(first, last, 6 // len(phases), body)
+
+    def edge_first(run, begin_swap):
+        for position, phase in ((0, 3), (1, 0)):
+
+            @pl.when(core == position)
+            def _(phase=phase):
+                run((phase,))
+
+        copy = begin_swap()
+        for position, phase in ((0, 0), (1, 3)):
+
+            @pl.when(core == position)
+            def _(phase=phase):
+                run((phase,))
+
+        return copy
 
     first = 1.0 + MOM + GAIN * (THETA - 1.0)
 
@@ -363,7 +379,7 @@
 
     setup_fine(INNER)
     copy.wait()
-    setup_fine(OUTER)
+    copy = edge_first(setup_fine, lambda: swap(xF, e1, 2, 20, WIN))
     for n, plane, condition in ((0, 2, gx == 0), (1, 17, gx == nx - 1)):
 
         @pl.when(condition)
@@ -379,11 +395,12 @@
                 for k in range(4):
                     gF[n, x, k, row : row + 1, :] = jnp.zeros((1, 128), F32)
 
-    copy = swap(xF, e1, 2, 20, WIN)
     sweep_fine(x2F, xF, e1, 2, 20, INNER, pre_step)
     copy.wait()
-    sweep_fine(x2F, xF, e1, 2, 20, OUTER, pre_step)
-    copy = swap(x2F, e2, 3, 19, WIN)
+    copy = edge_first(
+        lambda phases: sweep_fine(x2F, xF, e1, 2, 20, phases, pre_step),
+        lambda: swap(x2F, e2, 3, 19, WIN),
+    )
     sweep_fine(rF, x2F, e2, 3, 19, INNER, residual)
     copy.wait()
     sweep_fine(rF, x2F, e2, 3, 19, OUTER, residual)
@@ -397,39 +414,42 @@
                 for k in range(4):
                     rF[x, k, row : row + 4, :] = jnp.zeros((4, 128), F32)
 
-    def restrict_x(i):
-        results = [
-            0.125
-            * (
-                rF[2 * i, k, WIN, :]
-                + 3.0 * (rF[2 * i + 1, k, WIN, :] + rF[2 * i + 2, k, WIN, :])
-                + rF[2 * i + 3, k, WIN, :]
-            )
-            for k in range(4)
-        ]
-
-        def store_all():
-            for k in range(4):
-                t1[i, k, WIN, :] = results[k]
-
-        return store_all
-
-    def restrict_y(i):
-        results = []
-        for k in range(4):
-            part = [t1[i, k, pl.ds(s, 16, stride=2), :] for s in (11, 12, 13, 14)]
-            results.append(0.125 * (part[0] + 3.0 * (part[1] + part[2]) + part[3]))
-
-        def store_all():
-            for k in range(4):
-                t2[i, k] = results[k]
-
-        return store_all
-
-    planes(0, 10, 2, restrict_x)
-    planes(0, 10, 2, restrict_y)
-
+    def restrict_xy(phases):
+        def restrict_x(i):
+            results = [
+                0.125
+                * (
+                    rF[2 * i, k, WIN, :]
+                    + 3.0 * (rF[2 * i + 1, k, WIN, :] + rF[2 * i + 2, k, WIN, :])
+                    + rF[2 * i + 3, k, WIN, :]
+                )
+                for k in phases
+            ]
+
+            def store_all():
+                for k, value in zip(phases, results):
+                    t1[i, k, WIN, :] = value
+
+            return store_all
+
+        def restrict_y(i):
+            results = []
+            for k in phases:
+                part = [t1[i, k, pl.ds(s, 16, stride=2), :] for s in (11, 12, 13, 14)]
+                results.append(0.125 * (part[0] + 3.0 * (part[1] + part[2]) + part[3]))
+
+            def store_all():
+                for k, value in zip(phases, results):
+                    t2[i, k] = value
+
+            return store_all
+
+        planes(0, 10, 5, restrict_x)
+        planes(0, 10, 5, restrict_y)
+
+    restrict_xy(OUTER)
     copy = send(t2.at[:, edge_phase], e3.at[:, core], sibling)
+    restrict_xy(INNER)
     copy.wait()
     lane16 = lanes(16)
 
@@ -668,7 +688,7 @@
 
             return store_all
 
-        planes(number + 1, 19 - number, 4, body)
+        planes(number + 1, 19 - number, 6, body)
         now, later = later, now
     bottom = now
 
@@ -751,8 +771,10 @@
     copy = swap(cF, e1, 2, 20, WIN)
     sweep_fine(rF, cF, e1, 2, 20, INNER, last_first)
     copy.wait()
-    sweep_fine(rF, cF, e1, 2, 20, OUTER, last_first)
-    copy = swap(rF, e2, 3, 19, WIN)
+    copy = edge_first(
+        lambda phases: sweep_fine(rF, cF, e1, 2, 20, phases, last_first),
+        lambda: swap(rF, e2, 3, 19, WIN),
+    )
     sweep_fine(x2F, rF, e2, 3, 19, INNER, last_second)
     copy.wait()
     sweep_fine(x2F, rF, e2, 3, 19, OUTER, last_second)

time: 70.1 us -> 68.1 us (0.971)
  Pallas kernels: 70 us -> 68 us
    pallas_call x1, Pallas kernels: 67.9 us -> 65.9 us  [local(): pl.pallas_call(kernel, out_shape=jax.ShapeDtypeStruct((16, 32, 512), F32)...]
where the time goes in v3:
time: 68.1 us; the launch traced here: 68 us
  Pallas kernels  68 us (100%)
    pallas_call x1, Pallas kernels, local(): pl.pallas_call(kernel, out_shape=jax.ShapeDtypeStruct((16, 32, 512), F32)...  65.9 us
    pallas_call x1, Pallas kernels, local(): pl.pallas_call(copy_kernel, out_shape=jax.ShapeDtypeStruct((16, 32, 512),...  2.09 us

profile of v3, /device:TPU:1, one launch (start us, length us, event | category | flops | bytes accessed | tf_op | source)
XLA Modules:
  0.0 68.0 jit_solution(10386100976614038101)
XLA Ops:
  0.0 65.9 %shard_map.28.source = f32[16,32,512]{2,1,0:T(8,128)} custom-call(f32[16,32,512]{2,1,0:T(8,128)} %b_hbm.1, f32[16,32,512]{2,1,0:T(8,128)} %c_hbm.1), custom_call_target="tpu_custom_call" | custom-call | tf_op jit(solution)/shard_map/pallas_call | solution.py:835
  65.9 2.1 %shard_map.29 = f32[16,32,512]{2,1,0:T(8,128)} custom-call(f32[16,32,512]{2,1,0:T(8,128)} %shard_map.28.source), custom_call_target="tpu_custom_call" | custom-call | tf_op jit(solution)/shard_map/pallas_call | solution.py:845

commit v4 on v3

--- a/solution.py
+++ b/solution.py
@@ -453,13 +453,20 @@
     copy.wait()
     lane16 = lanes(16)
 
-    @pl.loop(0, 10)
-    def _(i):
+    def restrict_z(i):
         p = [t2[i, k] for k in range(4)]
         before = roll_up(jnp.where(lane16 == 127, e3[i, 0], p[3]))
         after = roll_down(jnp.where(lane16 == 0, e3[i, 1], p[0]))
-        b1[i + 3, 0, core, 16:32, :] = 0.125 * (before + 3.0 * (p[0] + p[1]) + p[2])
-        b1[i + 3, 1, core, 16:32, :] = 0.125 * (p[1] + 3.0 * (p[2] + p[3]) + after)
+        even = 0.125 * (before + 3.0 * (p[0] + p[1]) + p[2])
+        odd = 0.125 * (p[1] + 3.0 * (p[2] + p[3]) + after)
+
+        def store_all():
+            b1[i + 3, 0, core, 16:32, :] = even
+            b1[i + 3, 1, core, 16:32, :] = odd
+
+        return store_all
+
+    planes(0, 10, 5, restrict_z)
 
     halo_b1 = []
     for dx, dy in peers8:
@@ -611,18 +618,20 @@
 
     lane8 = lanes(8)
 
-    @pl.loop(0, 4)
-    def _(i):
+    for i in range(4):
+        for q in range(2):
+            for t in range(2):
+                t1[i, 2 * q + t, WL, :] = 0.125 * (
+                    xpL[2 * i + 3, q, t, WL, :]
+                    + 3.0 * (xpL[2 * i + 4, q, t, WL, :] + xpL[2 * i + 5, q, t, WL, :])
+                    + xpL[2 * i + 6, q, t, WL, :]
+                )
+    for i in range(4):
         coarse = []
         for q in range(2):
             halves = []
             for t in range(2):
-                tL[0, q, t, WL, :] = 0.125 * (
-                    xpL[2 * i + 3, q, t, WL, :]
-                    + 3.0 * (xpL[2 * i + 4, q, t, WL, :] + xpL[2 * i + 5, q, t, WL, :])
-                    + xpL[2 * i + 6, q, t, WL, :]
-                )
-                part = [tL[0, q, t, pl.ds(s, 8, stride=2), :] for s in (15, 16, 17, 18)]
+                part = [t1[i, 2 * q + t, pl.ds(s, 8, stride=2), :] for s in (15, 16, 17, 18)]
                 halves.append(0.125 * (part[0] + 3.0 * (part[1] + part[2]) + part[3]))
             coarse.append(halves)
         low, high = before_pair(coarse[1], lane8), after_pair(coarse[0], lane8)
@@ -655,13 +664,18 @@
     for copy in handed:
         copy.wait()
 
-    @pl.loop(0, 20)
-    def _(x):
-        for t in range(2):
-            scaled = jnp.where(c2[x, t, W2, :] > 0.0, bd2[x, t, W2, :], 0.0)
-            bd2[x, t, W2, :] = scaled
-            d2[x, t] = scaled * (1.0 / THETA_LOW)
-            xa[x, t, W2, :] = scaled * (1.0 / THETA_LOW)
+    def begin_low(x):
+        scaled = [jnp.where(c2[x, t, W2, :] > 0.0, bd2[x, t, W2, :], 0.0) for t in range(2)]
+
+        def store_all():
+            for t in range(2):
+                bd2[x, t, W2, :] = scaled[t]
+                d2[x, t] = scaled[t] * (1.0 / THETA_LOW)
+                xa[x, t, W2, :] = scaled[t] * (1.0 / THETA_LOW)
+
+        return store_all
+
+    planes(0, 20, 5, begin_low)
 
     now, later = xa, xb
     for number, (mom, gain) in enumerate(STEPS_LOW):
@@ -695,10 +709,9 @@
     for copy in far_mid:
         copy.wait()
 
-    @pl.loop(0, 8)
-    def _(i):
+    def prolong_mid(i):
+        results = []
         for odd in range(2):
-            x = 2 * i + odd
             mixed = [
                 0.75 * bottom[i + 6, t, W2, :] + 0.25 * bottom[i + 5 + 2 * odd, t, W2, :]
                 for t in range(2)
@@ -706,13 +719,45 @@
             low, high = before_pair(mixed, lane24), after_pair(mixed, lane24)
             for q, side in ((0, low), (1, high)):
                 for t in range(2):
-                    t3[odd, q, t, W2, :] = 0.75 * mixed[t] + 0.25 * side[t]
-                    centre = 0.75 * t3[odd, q, t, 12:28, :]
-                    x0L[x, q, t, pl.ds(8, 16, stride=2), :] = centre + 0.25 * t3[odd, q, t, 11:27, :]
-                    x0L[x, q, t, pl.ds(9, 16, stride=2), :] = centre + 0.25 * t3[odd, q, t, 13:29, :]
-                    x0L[x, q, t, WL, :] = jnp.where(
-                        c1[x, q, t, WL, :] > 0.0, x2L[x, q, t, WL, :] + x0L[x, q, t, WL, :], 0.0
-                    )
+                    results.append((odd, 2 * q + t, 0.75 * mixed[t] + 0.25 * side[t]))
+
+        def store_all():
+            for odd, slot, value in results:
+                bF[2 * i + odd, slot, W2, :] = value
+
+        return store_all
+
+    def prolong_mid_rows(x):
+        results = []
+        for slot in range(4):
+            centre = 0.75 * bF[x, slot, 12:28, :]
+            results.append(
+                (centre + 0.25 * bF[x, slot, 11:27, :], centre + 0.25 * bF[x, slot, 13:29, :])
+            )
+
+        def store_all():
+            for slot, (even, odd) in enumerate(results):
+                x0L[x, slot // 2, slot % 2, pl.ds(8, 16, stride=2), :] = even
+                x0L[x, slot // 2, slot % 2, pl.ds(9, 16, stride=2), :] = odd
+
+        return store_all
+
+    def correct_mid(x):
+        results = [
+            (q, t, jnp.where(c1[x, q, t, WL, :] > 0.0, x2L[x, q, t, WL, :] + x0L[x, q, t, WL, :], 0.0))
+            for q in range(2)
+            for t in range(2)
+        ]
+
+        def store_all():
+            for q, t, value in results:
+                x0L[x, q, t, WL, :] = value
+
+        return store_all
+
+    planes(0, 8, 2, prolong_mid)
+    planes(0, 16, 4, prolong_mid_rows)
+    planes(0, 16, 2, correct_mid)
 
     def post_first(x, q, t, total):
         start = x0L[x, q, t, WL, :]
@@ -734,10 +779,9 @@
     has_left = jnp.where(core == 1, 1.0, 0.0)
     has_right = jnp.where(core == 0, 1.0, 0.0)
 
-    @pl.loop(0, 10)
-    def _(i):
+    def prolong_fine(i):
+        results = []
         for odd in range(2):
-            x = 2 * i + 1 + odd
 
             def mixed(q, t):
                 return 0.75 * x2L[i + 3, q, t, WL, :] + 0.25 * x2L[i + 2 + 2 * odd, q, t, WL, :]
@@ -745,16 +789,45 @@
             m0, m1 = mixed(0, core), mixed(1, core)
             before = roll_up(jnp.where(lane32 == 127, has_left * mixed(1, other), m1))
             after = roll_down(jnp.where(lane32 == 0, has_right * mixed(0, other), m0))
-            fine = [
-                0.75 * m0 + 0.25 * before, 0.75 * m0 + 0.25 * m1,
-                0.75 * m1 + 0.25 * m0, 0.75 * m1 + 0.25 * after,
-            ]
+            results.append(
+                (
+                    0.75 * m0 + 0.25 * before, 0.75 * m0 + 0.25 * m1,
+                    0.75 * m1 + 0.25 * m0, 0.75 * m1 + 0.25 * after,
+                )
+            )
+
+        def store_all():
+            for odd in range(2):
+                for k in range(4):
+                    bF[2 * i + 1 + odd, k, WL, :] = results[odd][k]
+
+        return store_all
+
+    def prolong_fine_rows(x):
+        results = []
+        for k in range(4):
+            centre = 0.75 * bF[x, k, 14:34, :]
+            results.append((centre + 0.25 * bF[x, k, 13:33, :], centre + 0.25 * bF[x, k, 15:35, :]))
+
+        def store_all():
+            for k, (even, odd) in enumerate(results):
+                cF[x, k, pl.ds(8, 20, stride=2), :] = even
+                cF[x, k, pl.ds(9, 20, stride=2), :] = odd
+
+        return store_all
+
+    def correct_fine(x):
+        results = [cF[x, k, WIN, :] + x2F[x, k, WIN, :] for k in range(4)]
+
+        def store_all():
             for k in range(4):
-                tL[odd, k // 2, k % 2, WL, :] = fine[k]
-                centre = 0.75 * tL[odd, k // 2, k % 2, 14:34, :]
-                cF[x, k, pl.ds(8, 20, stride=2), :] = centre + 0.25 * tL[odd, k // 2, k % 2, 13:33, :]
-                cF[x, k, pl.ds(9, 20, stride=2), :] = centre + 0.25 * tL[odd, k // 2, k % 2, 15:35, :]
-                cF[x, k, WIN, :] = cF[x, k, WIN, :] + x2F[x, k, WIN, :]
+                cF[x, k, WIN, :] = results[k]
+
+        return store_all
+
+    planes(0, 10, 1, prolong_fine)
+    planes(1, 21, 2, prolong_fine_rows)
+    planes(1, 21, 2, correct_fine)
 
     def last_first(x, k, total):
         start = cF[x, k, WIN, :]

time: 68.1 us -> 67.2 us (0.987)
  Pallas kernels: 68 us -> 67.1 us
    pallas_call x1, Pallas kernels: 65.9 us -> 65 us  [local(): pl.pallas_call(kernel, out_shape=jax.ShapeDtypeStruct((16, 32, 512), F32)...]
where the time goes in v4:
time: 67.2 us; the launch traced here: 67.1 us
  Pallas kernels  67.1 us (100%)
    pallas_call x1, Pallas kernels, local(): pl.pallas_call(kernel, out_shape=jax.ShapeDtypeStruct((16, 32, 512), F32)...  65 us
    pallas_call x1, Pallas kernels, local(): pl.pallas_call(copy_kernel, out_shape=jax.ShapeDtypeStruct((16, 32, 512),...  2.09 us

profile of v4, /device:TPU:1, one launch (start us, length us, event | category | flops | bytes accessed | tf_op | source)
XLA Modules:
  0.0 67.1 jit_solution(579397190166037767)
XLA Ops:
  0.0 65.0 %shard_map.28.source = f32[16,32,512]{2,1,0:T(8,128)} custom-call(f32[16,32,512]{2,1,0:T(8,128)} %b_hbm.1, f32[16,32,512]{2,1,0:T(8,128)} %c_hbm.1), custom_call_target="tpu_custom_call" | custom-call | tf_op jit(solution)/shard_map/pallas_call | solution.py:908
  65.0 2.1 %shard_map.29 = f32[16,32,512]{2,1,0:T(8,128)} custom-call(f32[16,32,512]{2,1,0:T(8,128)} %shard_map.28.source), custom_call_target="tpu_custom_call" | custom-call | tf_op jit(solution)/shard_map/pallas_call | solution.py:918

commit v5 on v4

--- a/solution.py
+++ b/solution.py
@@ -335,7 +335,7 @@
 
             return store_all
 
-        planes(first, last, 6 // len(phases), body)
+        planes(first, last, (8 if (last - first) % 8 == 0 else 6) // len(phases), body)
 
     def edge_first(run, begin_swap):
         for position, phase in ((0, 3), (1, 0)):
@@ -557,10 +557,16 @@
     setup_low(8, 12)
 
     def scale_mid(first, last):
-        @pl.loop(first, last)
-        def _(x):
-            for q in range(2):
-                x1L[x, q, core, WL, :] = b1[x, q, core, WL, :] * x0L[x, q, core, WL, :]
+        def body(x):
+            results = [b1[x, q, core, WL, :] * x0L[x, q, core, WL, :] for q in range(2)]
+
+            def store_all():
+                for q in range(2):
+                    x1L[x, q, core, WL, :] = results[q]
+
+            return store_all
+
+        planes(first, last, 2, body)
 
         return send(
             x1L.at[first:last, :, core, 8:40], x1L.at[first:last, :, core, 8:40], sibling

time: 67.2 us -> 67.2 us (level)
  no operation moved by 1% of the time
where the time goes in v5:
time: 67.2 us; the launch traced here: 67.1 us
  Pallas kernels  67.1 us (100%)
    pallas_call x1, Pallas kernels, local(): pl.pallas_call(kernel, out_shape=jax.ShapeDtypeStruct((16, 32, 512), F32)...  65 us
    pallas_call x1, Pallas kernels, local(): pl.pallas_call(copy_kernel, out_shape=jax.ShapeDtypeStruct((16, 32, 512),...  2.09 us

profile of v5, /device:TPU:1, one launch (start us, length us, event | category | flops | bytes accessed | tf_op | source)
XLA Modules:
  0.0 67.1 jit_solution(6757433591685454709)
XLA Ops:
  0.0 65.0 %shard_map.28.source = f32[16,32,512]{2,1,0:T(8,128)} custom-call(f32[16,32,512]{2,1,0:T(8,128)} %b_hbm.1, f32[16,32,512]{2,1,0:T(8,128)} %c_hbm.1), custom_call_target="tpu_custom_call" | custom-call | tf_op jit(solution)/shard_map/pallas_call | solution.py:914
  65.0 2.1 %shard_map.29 = f32[16,32,512]{2,1,0:T(8,128)} custom-call(f32[16,32,512]{2,1,0:T(8,128)} %shard_map.28.source), custom_call_target="tpu_custom_call" | custom-call | tf_op jit(solution)/shard_map/pallas_call | solution.py:924

commit v6 on v4

--- a/solution.py
+++ b/solution.py
@@ -97,10 +97,6 @@
         send(c_hbm.at[0:3], face_c_in.at[1], peer(-1, 0)),
         send(c_hbm.at[13:16], face_c_in.at[0], peer(1, 0)),
     ]
-    face_b = [
-        send(b_hbm.at[0:2], face_b_in.at[1], peer(-1, 0)),
-        send(b_hbm.at[14:16], face_b_in.at[0], peer(1, 0)),
-    ]
     load_c.wait()
     load_b.wait()
 
@@ -117,6 +113,10 @@
         send(pk_out.at[0, 13:16], pk_in.at[1, 0:3], peer(1, -1)),
         send(pk_out.at[1, 0:3], pk_in.at[0, 19:22], peer(-1, 1)),
         send(pk_out.at[1, 13:16], pk_in.at[0, 0:3], peer(1, 1)),
+    ]
+    face_b = [
+        send(b_hbm.at[0:2], face_b_in.at[1], peer(-1, 0)),
+        send(b_hbm.at[14:16], face_b_in.at[0], peer(1, 0)),
     ]
 
     @pl.loop(0, 4)
@@ -187,9 +187,6 @@
     for copy in face_c:
         copy.wait_recv()
     spread_faces(face_c_in, cF, 3, 0, 19)
-    for copy in face_b:
-        copy.wait_recv()
-    spread_faces(face_b_in, bF, 2, 1, 19)
     for copy in halo:
         copy.wait_recv()
     for side in range(2):
@@ -377,6 +374,9 @@
         for dx, dy in peers14
     ]
 
+    for face in face_b:
+        face.wait_recv()
+    spread_faces(face_b_in, bF, 2, 1, 19)
     setup_fine(INNER)
     copy.wait()
     copy = edge_first(setup_fine, lambda: swap(xF, e1, 2, 20, WIN))

time: 67.2 us -> 65.1 us (0.969)
  Pallas kernels: 67.1 us -> 65 us
    pallas_call x1, Pallas kernels: 65 us -> 62.9 us  [local(): pl.pallas_call(kernel, out_shape=jax.ShapeDtypeStruct((16, 32, 512), F32)...]
where the time goes in v6:
time: 65.1 us; the launch traced here: 65 us
  Pallas kernels  65 us (100%)
    pallas_call x1, Pallas kernels, local(): pl.pallas_call(kernel, out_shape=jax.ShapeDtypeStruct((16, 32, 512), F32)...  62.9 us
    pallas_call x1, Pallas kernels, local(): pl.pallas_call(copy_kernel, out_shape=jax.ShapeDtypeStruct((16, 32, 512),...  2.09 us

profile of v6, /device:TPU:1, one launch (start us, length us, event | category | flops | bytes accessed | tf_op | source)
XLA Modules:
  0.0 65.0 jit_solution(5956806546172737471)
XLA Ops:
  0.0 62.9 %shard_map.28.source = f32[16,32,512]{2,1,0:T(8,128)} custom-call(f32[16,32,512]{2,1,0:T(8,128)} %b_hbm.1, f32[16,32,512]{2,1,0:T(8,128)} %c_hbm.1), custom_call_target="tpu_custom_call" | custom-call | tf_op jit(solution)/shard_map/pallas_call | solution.py:908
  62.9 2.1 %shard_map.29 = f32[16,32,512]{2,1,0:T(8,128)} custom-call(f32[16,32,512]{2,1,0:T(8,128)} %shard_map.28.source), custom_call_target="tpu_custom_call" | custom-call | tf_op jit(solution)/shard_map/pallas_call | solution.py:918
